TPU v7x, 256 devices: a whole 4x4x8 slice. The times are simulated.
256 devices in a mesh: row: 16 (over x, y), col: 16 (over z, core).
Axes of the slice: x: 4, y: 4, z: 8, core: 2. Of those that a mesh axis runs over, the one named last changes fastest.
Arguments:
- source: float32 [8, 8192, 4096], P(None, 'col', 'row'), may hold values from -6 to 6
- pole_x: float32 [8, 4], replicated, may hold values from 0.95 to 1, as said below
- weight_x: float32 [8, 4], replicated, may hold values from 0.15 to 0.4
- pole_y: float32 [8, 4], replicated, may hold values from 0.95 to 1, as said below
- weight_y: float32 [8, 4], replicated, may hold values from 0.15 to 0.4
Outputs:
- coefficient: float32 [8, 8192, 4096], P(None, 'col', 'row')
Inputs may be any that keep to these rules, and one draw needn't show every extreme that they name: `pole_x`: each pole is below one. `pole_y`: each pole is below one.
All inputs are finite; a program needn't handle non-finite values.
Results may differ from a plain program's by a relative error of at most 0.0003.
Values sent between devices are 32-bit elements; how exact they have to be, the bound alone decides.
A program may use at most 128 MiB of HBM per device.

v0:
```python
import jax
import jax.numpy as jnp
from jax import lax
from jax.sharding import PartitionSpec as P

highest = lax.Precision.HIGHEST


def prefix(value, axis, join, neutral, backward):
    count, mine = (lax.axis_size(axis), lax.axis_index(axis))
    pieces = jax.tree.map(lambda part: lax.all_gather(part, axis), value)
    if backward:
        pieces = jax.tree.map(lambda part: part[::-1], pieces)
        mine = count - 1 - mine
    subtotal = jax.tree.map(
        lambda part, zero: jnp.full_like(part, 0) + jnp.asarray(zero, part.dtype), value, neutral
    )

    def lap(position, subtotal):
        longer = join(subtotal, jax.tree.map(lambda part: part[position], pieces))
        return jax.tree.map(lambda new, old: jnp.where(position < mine, new, old), longer, subtotal)

    return lax.fori_loop(0, count - 1, lap, subtotal)


def block_tables(pole_values, weights, block_len, forward):
    log_pole = jnp.log(pole_values)
    places = jnp.arange(block_len, dtype=jnp.float32)
    if forward:
        gain_rate = jnp.sqrt(1.0 - pole_values * pole_values)
        offset = places[:, None] - places[None, :]
        state_expo = block_len - 1.0 - places
        carry_expo = places + 1.0
    else:
        gain_rate = 1.0 - pole_values
        offset = places[None, :] - places[:, None]
        state_expo = places
        carry_expo = block_len - places
    inside = offset >= 0.0
    decays = jnp.exp(log_pole[:, :, None, None] * jnp.maximum(offset, 0.0))
    decays = jnp.where(inside, decays, 0.0)
    matrix = jnp.einsum("lk,lkab->lab", weights * gain_rate, decays, precision=highest)
    state_map = gain_rate[:, :, None] * jnp.exp(log_pole[:, :, None] * state_expo[None, None, :])
    carry_map = weights[:, None, :] * jnp.exp(log_pole[:, None, :] * carry_expo[None, :, None])
    return (matrix, state_map, carry_map)


def chain_tables(pole_values, block_len, blocks, forward):
    step_log = jnp.log(pole_values) * block_len
    positions = jnp.arange(blocks, dtype=jnp.float32)
    if forward:
        distance = positions[:, None] - 1.0 - positions[None, :]
        summary_expo = blocks - 1.0 - positions
        entry_expo = positions
    else:
        distance = positions[None, :] - 1.0 - positions[:, None]
        summary_expo = positions
        entry_expo = blocks - 1.0 - positions
    spread = jnp.exp(step_log[:, :, None, None] * jnp.maximum(distance, 0.0))
    spread = jnp.where(distance >= 0.0, spread, 0.0)
    summary_w = jnp.exp(step_log[:, :, None] * summary_expo[None, None, :])
    entry_w = jnp.exp(step_log[:, :, None] * entry_expo[None, None, :])
    return (spread, summary_w, entry_w)


def line_local(field_in, pole_values, weights, line_dim, forward):
    levels, middle_size, inner_size = field_in.shape
    length = field_in.shape[line_dim]
    block_len = 128
    blocks = length // block_len
    matrix, state_map, carry_map = block_tables(pole_values, weights, block_len, forward)
    spread, summary_w, entry_w = chain_tables(pole_values, block_len, blocks, forward)
    if line_dim == 2:
        blocked = field_in.reshape(levels, middle_size, blocks, block_len)
        local_part = jnp.einsum("lab,lmcb->lmca", matrix, blocked, precision=highest)
        states = jnp.einsum("lkb,lmcb->lckm", state_map, blocked, precision=highest)
    else:
        blocked = field_in.reshape(levels, blocks, block_len, inner_size)
        local_part = jnp.einsum("lab,lcbm->lcam", matrix, blocked, precision=highest)
        states = jnp.einsum("lkb,lcbm->lckm", state_map, blocked, precision=highest)
    inner_carry = jnp.einsum("lkcd,ldkm->lckm", spread, states, precision=highest)
    summary = jnp.einsum("lkc,lckm->lkm", summary_w, states, precision=highest)
    return (local_part, inner_carry, summary, (carry_map, entry_w))


def line_finish(local_part, inner_carry, tables, incoming, line_dim, shape_out):
    carry_map, entry_w = tables
    carries = inner_carry + jnp.swapaxes(entry_w, 1, 2)[:, :, :, None] * incoming[:, None, :, :]
    if line_dim == 2:
        fixed = local_part + jnp.einsum("lak,lckm->lmca", carry_map, carries, precision=highest)
    else:
        fixed = local_part + jnp.einsum("lak,lckm->lcam", carry_map, carries, precision=highest)
    return fixed.reshape(shape_out)


def join_segments(earlier, later_part):
    return (earlier[0] * later_part[0], later_part[0] * earlier[1] + later_part[1])


def on_device(source, pole_x, weight_x, pole_y, weight_y):
    levels, rows_here, cols_here = source.shape
    pole_count = pole_x.shape[1]
    line_rows = lax.all_to_all(source, "row", split_axis=1, concat_axis=2, tiled=True)
    zero_in = jnp.zeros((levels, pole_count, line_rows.shape[1]), jnp.float32)
    local_part, inner_carry, summary, tables = line_local(line_rows, pole_x, weight_x, 2, True)
    along_x = line_finish(local_part, inner_carry, tables, zero_in, 2, line_rows.shape)
    local_part, inner_carry, summary, tables = line_local(along_x, pole_x, weight_x, 2, False)
    smooth_lines = line_finish(local_part, inner_carry, tables, zero_in, 2, line_rows.shape)
    smooth_x = lax.all_to_all(smooth_lines, "row", split_axis=2, concat_axis=1, tiled=True)
    decay_y = jnp.exp(jnp.log(pole_y) * rows_here)[:, :, None]
    identity = (jnp.ones_like(decay_y), jnp.zeros((levels, pole_count, cols_here), jnp.float32))
    local_part, inner_carry, summary, tables = line_local(smooth_x, pole_y, weight_y, 1, True)
    from_below = prefix((decay_y, summary), "col", join_segments, identity, False)[1]
    along_y = line_finish(local_part, inner_carry, tables, from_below, 1, smooth_x.shape)
    local_part, inner_carry, summary, tables = line_local(along_y, pole_y, weight_y, 1, False)
    from_above = prefix((decay_y, summary), "col", join_segments, identity, True)[1]
    smooth_y = line_finish(local_part, inner_carry, tables, from_above, 1, smooth_x.shape)
    return jnp.exp(smooth_y)


def solution(mesh):
    return jax.shard_map(
        on_device,
        mesh=mesh,
        in_specs=(P(None, "col", "row"), P(), P(), P(), P()),
        out_specs=P(None, "col", "row"),
        check_vma=False,
    )
```

profile of v0, /device:TPU:1, one launch (start us, length us, event | category | flops | bytes accessed | tf_op | source)
XLA Modules:
  0.0 365.1 jit_solution(4943154217428443616)
XLA Ops:
  0.0 6.6 %copy.97 = f32[8,512,256]{2,0,1:T(8,128)} copy(f32[8,512,256]{2,1,0:T(8,128)} %param.9) | data formatting | bytes 8388608 | tf_op args[0]
  6.6 8.0 %all-to-all-start = ((f32[8,512,256]{2,0,1:T(8,128)}), f32[8,512,256]{2,0,1:T(8,128)}, u32[]{:S(2)}, u32[]{:S(2)}) async-start(f32[8,512,256]{2,0,1:T(8,128)} %copy.97), calls=%async_computation | async-start | bytes 8388608 | tf_op jit(solution)/shard_map/all_to_all | solution.py:103
  15.7 2.6 exponential_select_fusion.2
  18.2 4.3 %fusion.10 = f32[8,1,128,128]{3,1,2,0:T(1,128)S(1)} fusion(f32[8,4,1,1]{1,2,3,0:T(1,128)S(1)} %copy.137, f32[8,4,128,128]{3,2,1,0:T(8,128)S(1)} %get-tuple-element.293), kind=kOutput, calls=%fused_computation.19 | convolution fusion | flops 6291456 | bytes 2621568 | tf_op jit(solution)/shard_map/lk,lkab->lab/dot_general | solution.py:42
  22.5 4.3 %fusion.12 = f32[8,1,128,128]{3,1,2,0:T(1,128)S(1)} fusion(f32[8,4,1,1]{1,2,3,0:T(1,128)S(1)} %copy.131, f32[8,4,128,128]{3,2,1,0:T(8,128)S(1)} %get-tuple-element.295), kind=kOutput, calls=%fused_computation.21 | convolution fusion | flops 6291456 | bytes 2621568 | tf_op jit(solution)/shard_map/lk,lkab->lab/dot_general | solution.py:42
  26.8 48.6 %all-to-all-done = f32[8,512,256]{2,0,1:T(8,128)} async-done(((f32[8,512,256]{2,0,1:T(8,128)}), f32[8,512,256]{2,0,1:T(8,128)}, u32[]{:S(2)}, u32[]{:S(2)}) %all-to-all-start) | async-done | bytes 4194336 | tf_op jit(solution)/shard_map/all_to_all | solution.py:103
  75.4 6.6 %copy.196 = f32[8,16,32,256]{3,1,2,0:T(8,128)} copy(f32[8,16,32,256]{3,0,2,1:T(8,128)} %bitcast.5) | data formatting | bytes 8388608 | tf_op jit(solution)/shard_map/all_to_all | solution.py:103
  82.0 4.7 %reshape.193 = f32[8,32,32,128]{3,2,1,0:T(8,128)} reshape(f32[8,32,16,256]{3,2,1,0:T(8,128)} %bitcast.185) | data formatting | bytes 8388608 | tf_op jit(solution)/shard_map/reshape | solution.py:74
  86.7 5.7 %fusion.133 = f32[8,128,32,32]{1,3,2,0:T(8,128)S(1)} fusion(f32[8,128,128,1]{2,1,3,0:T(8,128)S(1)} %bitcast.189, f32[8,32,32,128]{3,2,1,0:T(8,128)} %reshape.193), kind=kOutput, calls=%fused_computation.184 | convolution fusion | flops 1610612736 | bytes 8912896 | tf_op jit(solution)/shard_map/lab,lmcb->lmca/dot_general | solution.py:75
  92.5 16.3 %convolution_bitcast_fusion.1 = f32[8,32,4,32]{1,2,3,0:T(4,128)S(1)} fusion(f32[8,32,32,128]{3,2,1,0:T(8,128)S(1)} %copy-done.1, f32[128]{0:T(128)S(1)} %iota_subtract_fusion.9, f32[8,4]{1,0:T(8,128)S(1)} %copy.96, f32[8,4]{1,0:T(8,128)S(1)} %copy.99), kind=kOutput, calls=%fused_computation.28 | convolution fusion | flops 50339840 | bytes 4326144 | tf_op jit(solution)/shard_map/lkb,lmcb->lckm/dot_general | solution.py:76
  108.8 1.1 fusion.15
  109.9 7.2 %bitcast_add_fusion.3 = f32[8,32,32,128]{3,2,1,0:T(8,128)S(1)} fusion(f32[8,128,32,32]{1,3,2,0:T(8,128)S(1)} %fusion.133, f32[8,32,4,32]{1,3,2,0:T(8,128)S(1)} %fusion.15, f32[128]{0:T(128)S(1)} %iota_add_fusion.1, f32[8,4]{1,0:T(8,128)S(1)} %copy.96, f32[8,4]{1,0:T(8,128)S(1)} %copy.104), kind=kOutput, calls=%fused_computation.11 | convolution fusion | flops 51388416 | bytes 8520448 | tf_op jit(solution)/shard_map/lak,lckm->lmca/dot_general | solution.py:90
  117.2 16.3 %convolution_bitcast_fusion = f32[8,32,4,32]{1,2,3,0:T(4,128)S(1)} fusion(f32[8,32,32,128]{3,2,1,0:T(8,128)S(1)} %bitcast_add_fusion.3, f32[8,4]{1,0:T(8,128)S(1)} %copy.107, f32[8,4]{1,0:T(8,128)S(1)} %copy.96), kind=kOutput, calls=%fused_computation.27 | convolution fusion | flops 50339840 | bytes 4325632 | tf_op jit(solution)/shard_map/lkb,lmcb->lckm/dot_general | solution.py:76
  133.5 4.5 %fusion.134 = f32[8,32,32,128]{3,2,1,0:T(8,128)S(1)} fusion(f32[8,32,32,128]{3,2,1,0:T(8,128)S(1)} %bitcast_add_fusion.3, f32[8,128,128,1]{2,1,3,0:T(8,128)S(1)} %bitcast.187), kind=kOutput, calls=%fused_computation.185 | convolution fusion | flops 1610612736 | bytes 8912896 | tf_op jit(solution)/shard_map/lab,lmcb->lmca/dot_general | solution.py:75
  138.0 1.1 fusion.14
  139.1 8.4 %bitcast_add_fusion.2 = f32[8,32,32,128]{3,2,1,0:T(8,128)} fusion(f32[8,32,32,128]{3,2,1,0:T(8,128)S(1)} %fusion.134, f32[8,32,4,32]{1,3,2,0:T(8,128)S(1)} %fusion.14, f32[128]{0:T(128)S(1)} %iota_subtract_fusion.7, f32[8,4]{1,0:T(8,128)S(1)} %copy.96, f32[8,4]{1,0:T(8,128)S(1)} %copy.104), kind=kOutput, calls=%fused_computation.10 | convolution fusion | flops 51388416 | bytes 8520448 | tf_op jit(solution)/shard_map/lak,lckm->lmca/dot_general | solution.py:90
  147.5 9.4 %copy.162 = f32[8,32,32,128]{1,0,3,2:T(8,128)} copy(f32[8,32,32,128]{3,2,1,0:T(8,128)} %bitcast_add_fusion.2) | data formatting | bytes 8388608 | tf_op jit(solution)/shard_map/reshape | solution.py:93
  156.9 16.0 %reshape.227 = f32[16,1,65536]{2,1,0:T(1,128)} reshape(f32[4096,8,32]{2,1,0:T(8,128)} %bitcast.181) | data formatting | bytes 8388608
  172.9 10.8 %all-to-all-start.1 = ((f32[16,1,65536]{2,1,0:T(1,128)}), f32[16,1,65536]{2,1,0:T(1,128)}, u32[]{:S(2)}, u32[]{:S(2)}) async-start(f32[16,1,65536]{2,1,0:T(1,128)} %reshape.227), calls=%async_computation.1 | async-start | bytes 8388608 | tf_op jit(solution)/shard_map/all_to_all | solution.py:109
  184.2 22.2 %all-gather.3 = f32[16,8,4]{1,2,0:T(4,128)S(1)} all-gather(f32[1,8,4]{1,2,0:T(4,128)S(1)} %get-tuple-element.309), channel_id=2, replica_groups=mesh['row'=16,'col'=16] {'col'}, dimensions={0}, use_global_device_ids=true | all-gather | bytes 2176 | tf_op jit(solution)/shard_map/all_gather | solution.py:11
  206.8 6.6 %fusion.6 = f32[8,1,128,128]{3,1,2,0:T(1,128)S(1)} fusion(f32[8,4,1,1]{1,2,3,0:T(1,128)S(1)} %copy.152, f32[8,4,128,128]{3,2,1,0:T(8,128)} %get-tuple-element.294), kind=kOutput, calls=%fused_computation.15 | convolution fusion | flops 6291456 | bytes 2621568 | tf_op jit(solution)/shard_map/lk,lkab->lab/dot_general | solution.py:42
  213.4 4.7 %fusion.8 = f32[8,1,128,128]{3,1,2,0:T(1,128)S(1)} fusion(f32[8,4,1,1]{1,2,3,0:T(1,128)S(1)} %copy.143, f32[8,4,128,128]{3,2,1,0:T(8,128)S(1)} %get-tuple-element.296), kind=kOutput, calls=%fused_computation.17 | convolution fusion | flops 6291456 | bytes 2621568 | tf_op jit(solution)/shard_map/lk,lkab->lab/dot_general | solution.py:42
  218.1 16.9 %all-to-all-done.1 = f32[16,1,65536]{2,1,0:T(1,128)} async-done(((f32[16,1,65536]{2,1,0:T(1,128)}), f32[16,1,65536]{2,1,0:T(1,128)}, u32[]{:S(2)}, u32[]{:S(2)}) %all-to-all-start.1) | async-done | bytes 4194336 | tf_op jit(solution)/shard_map/all_to_all | solution.py:109
  235.0 0.6 broadcast.274
  235.5 13.8 %reduce = f32[16,65536]{1,0:T(8,128)} reduce(f32[16,1,65536]{2,1,0:T(1,128)} %all-to-all-done.1, f32[]{:T(128)} %broadcast.274), dimensions={1}, to_apply=%all_to_all.25.reduce_sub_computation | reduce | bytes 8388612 | tf_op jit(solution)/shard_map/all_to_all | solution.py:109
  249.3 15.1 %reshape.228 = f32[4096,8,32]{2,1,0:T(8,128)} reshape(f32[16,65536]{1,0:T(8,128)} %reduce) | data formatting | bytes 8388608
  264.4 11.4 %copy.112 = f32[8,16,32,256]{3,2,1,0:T(8,128)} copy(f32[8,16,32,256]{2,0,3,1:T(8,128)} %bitcast.182) | data formatting | bytes 8388608 | tf_op jit(solution)/shard_map/all_to_all | solution.py:109
  275.8 4.6 %convolution_bitcast_fusion.6 = f32[8,4,4,256]{3,2,1,0:T(4,128)S(1)} fusion(f32[8,4,128,256]{3,2,1,0:T(8,128)} %bitcast.183, f32[8,4]{1,0:T(8,128)S(1)} %copy.113, f32[8,4]{1,0:T(8,128)S(1)} %copy.115, f32[128]{0:T(128)S(1)} %iota_subtract_fusion.9), kind=kOutput, calls=%fused_computation.38 | convolution fusion | flops 50339840 | bytes 4326144 | tf_op jit(solution)/shard_map/lkb,lcbm->lckm/dot_general | solution.py:80
  280.4 8.3 %fusion.135 = f32[8,4,256,128]{3,2,1,0:T(8,128)} fusion(f32[8,4,128,256]{3,2,1,0:T(8,128)S(1)} %bitcast.184, f32[8,128,128,1]{2,1,3,0:T(8,128)S(1)} %bitcast.188), kind=kOutput, calls=%fused_computation.186 | convolution fusion | flops 1610612736 | bytes 8912896 | tf_op jit(solution)/shard_map/lab,lcbm->lcam/dot_general | solution.py:79
  288.7 0.4 fusion.44
  289.1 26.7 %all-gather.1 = f32[128,4,256]{2,1,0:T(4,128)S(1)} all-gather(f32[8,4,256]{2,1,0:T(4,128)S(1)} %bitcast.193), channel_id=3, replica_groups=mesh['row'=16,'col'=16] {'col'}, dimensions={0}, use_global_device_ids=true | all-gather | bytes 557056 | tf_op jit(solution)/shard_map/all_gather | solution.py:11
  315.8 3.3 while.28
  316.1 0.1 fusion.154
  316.3 0.1 fusion.154
  316.5 0.1 fusion.154
  316.7 0.1 fusion.154
  316.9 0.1 fusion.154
  317.1 0.1 fusion.154
  317.3 0.1 fusion.154
  317.6 0.1 fusion.154
  317.8 0.1 fusion.154
  318.0 0.1 fusion.154
  318.2 0.1 fusion.154
  318.4 0.1 fusion.154
  318.6 0.1 fusion.154
  318.8 0.1 fusion.154
  319.0 0.1 fusion.154
  319.1 0.4 fusion.17
  319.6 8.5 %convolution_add_fusion = f32[8,4,256,128]{3,2,1,0:T(8,128)S(1)} fusion(f32[8,4,256,128]{3,2,1,0:T(8,128)} %fusion.135, f32[8,4,4,256]{3,1,2,0:T(4,128)S(1)} %fusion.17, f32[8,4]{1,0:T(8,128)S(1)} %copy.113, f32[8,4]{1,0:T(8,128)S(1)} %copy.122, f32[128]{0:T(128)S(1)} %iota_add_fusion.1), kind=kOutput, calls=%fused_computation.14 | convolution fusion | flops 51388416 | bytes 8520448 | tf_op jit(solution)/shard_map/lak,lckm->lcam/dot_general | solution.py:92
  328.1 3.6 fusion.18
  331.7 5.9 %fusion.4 = f32[8,4,256,128]{2,3,1,0:T(8,128)} fusion(f32[8,128,128,1]{2,1,3,0:T(8,128)S(1)} %bitcast.186, f32[8,4,256,128]{3,2,1,0:T(8,128)S(1)} %convolution_add_fusion), kind=kOutput, calls=%fused_computation.8 | convolution fusion | flops 1610612736 | bytes 8912896 | tf_op jit(solution)/shard_map/lab,lcbm->lcam/dot_general | solution.py:79
  337.6 0.4 fusion.41
  338.0 15.9 %all-gather.2 = f32[128,4,256]{2,1,0:T(4,128)S(1)} all-gather(f32[8,4,256]{2,1,0:T(4,128)S(1)} %bitcast.194), channel_id=4, replica_groups=mesh['row'=16,'col'=16] {'col'}, dimensions={0}, use_global_device_ids=true | all-gather | bytes 557056 | tf_op jit(solution)/shard_map/all_gather | solution.py:11
  353.9 3.1 while.29
  354.1 0.1 fusion.155
  354.3 0.1 fusion.155
  354.5 0.1 fusion.155
  354.7 0.1 fusion.155
  354.9 0.1 fusion.155
  355.1 0.1 fusion.155
  355.3 0.1 fusion.155
  355.5 0.1 fusion.155
  357.1 0.4 fusion.16
  357.5 7.5 %add_exponential_fusion = f32[8,4,256,128]{2,3,1,0:T(8,128)} fusion(f32[8,4,256,128]{2,3,1,0:T(8,128)} %fusion.4, f32[8,4,4,256]{3,1,2,0:T(4,128)S(1)} %fusion.16, f32[8,4]{1,0:T(8,128)S(1)} %copy.113, f32[8,4]{1,0:T(8,128)S(1)} %copy.122, f32[128]{0:T(128)S(1)} %iota_subtract_fusion.7), kind=kOutput, calls=%fused_computation.13 | convolution fusion | flops 51388416 | bytes 8520448 | tf_op jit(solution)/shard_map/lak,lckm->lcam/dot_general | solution.py:92
  (117 shorter events, 5.3 us)
Async XLA Ops:
  6.6 8.0 %copy-start.3 = (f32[8,4]{0,1:T(4,128)S(1)}, f32[8,4]{0,1:T(4,128)}, u32[]{:S(2)}) copy-start(f32[8,4]{0,1:T(4,128)} %param.11) | copy-start | bytes 388
  6.6 8.1 %copy-start.5 = (f32[8,4]{0,1:T(4,128)S(1)}, f32[8,4]{0,1:T(4,128)}, u32[]{:S(2)}) copy-start(f32[8,4]{0,1:T(4,128)} %param.10) | copy-start | bytes 388
  6.6 8.6 %copy-start.2 = (f32[8,4]{0,1:T(4,128)S(1)}, f32[8,4]{0,1:T(4,128)}, u32[]{:S(2)}) copy-start(f32[8,4]{0,1:T(4,128)} %param.13) | copy-start | bytes 388
  6.6 8.6 %copy-start.4 = (f32[8,4]{0,1:T(4,128)S(1)}, f32[8,4]{0,1:T(4,128)}, u32[]{:S(2)}) copy-start(f32[8,4]{0,1:T(4,128)} %param.12) | copy-start | bytes 388
  6.6 68.7 %all-to-all-start = ((f32[8,512,256]{2,0,1:T(8,128)}), f32[8,512,256]{2,0,1:T(8,128)}, u32[]{:S(2)}, u32[]{:S(2)}) async-start(f32[8,512,256]{2,0,1:T(8,128)} %copy.97), calls=%async_computation | async-start | bytes 8388608 | tf_op jit(solution)/shard_map/all_to_all | solution.py:103
  86.7 5.8 %copy-start.1 = (f32[8,32,32,128]{3,2,1,0:T(8,128)S(1)}, f32[8,32,32,128]{3,2,1,0:T(8,128)}, u32[]{:S(2)}) copy-start(f32[8,32,32,128]{3,2,1,0:T(8,128)} %reshape.193) | copy-start | bytes 12582916
  172.9 62.0 %all-to-all-start.1 = ((f32[16,1,65536]{2,1,0:T(1,128)}), f32[16,1,65536]{2,1,0:T(1,128)}, u32[]{:S(2)}, u32[]{:S(2)}) async-start(f32[16,1,65536]{2,1,0:T(1,128)} %reshape.227), calls=%async_computation.1 | async-start | bytes 8388608 | tf_op jit(solution)/shard_map/all_to_all | solution.py:109
  275.8 4.6 %copy-start = (f32[8,16,32,256]{3,2,1,0:T(8,128)S(1)}, f32[8,16,32,256]{3,2,1,0:T(8,128)}, u32[]{:S(2)}) copy-start(f32[8,16,32,256]{3,2,1,0:T(8,128)} %copy.112) | copy-start | bytes 12582916
where the time goes:
time: 369 us; the launch traced here: 365 us
  matrix products  120 us (33%)
  local copies, waits for them, and re-layouts  74.4 us (20%)
  waiting for transfers between devices  65.5 us (18%)
  blocking collectives  64.9 us (18%)
  other arithmetic  19.7 us (5%)
  starting transfers between devices  18.8 us (5%)
    all_gather x3, blocking collectives, prefix(): pieces = jax.tree.map(lambda part: lax.all_gather(part, axis), value)  64.9 us
    all_to_all x1, waiting for transfers between devices, on_device(): lax.all_to_all(source, 'row', split_axis=1, concat_axis=2, tiled=True)  48.6 us
    unnamed x18, local copies, waits for them, and re-layouts  37.9 us
    dot_general x2, matrix products, line_local(): states = jnp.einsum('lkb,lmcb->lckm', state_map, blocked, precision=highest)  32.6 us
    dot_general x4, matrix products, block_tables(): jnp.einsum('lk,lkab->lab', weights * gain_rate, decays, precision=highest)  19.8 us
    all_to_all x1, waiting for transfers between devices, on_device(): lax.all_to_all(smooth_lines, 'row', split_axis=2, concat_axis=1, tiled=True)  16.9 us
    dot_general x2, matrix products, line_finish(): jnp.einsum('lak,lckm->lcam', carry_map, carries, precision=highest)  16 us
    dot_general x2, matrix products, line_finish(): jnp.einsum('lak,lckm->lmca', carry_map, carries, precision=highest)  15.7 us
  transfers between devices with their start and end apart: 2, of which 2 were waited for; matrix products, arithmetic and copies ran while one was open for 7% of the time, Pallas kernels for 0%

commit v1 on v0

v1 whole, which is shorter than its diff:
```python
import functools

import jax
import jax.numpy as jnp
from jax import lax
from jax.experimental import pallas as pl
from jax.experimental.pallas import tpu as pltpu
from jax.sharding import PartitionSpec as P

MESH = pl.DeviceIdType.MESH
LEVELS = 8
POLES = 4
BLOCK = 256
PEERS = 16
f32 = jnp.float32
bf16 = jnp.bfloat16
NN = (((1,), (0,)), ((), ()))
NT = (((1,), (1,)), ((), ()))
TN = (((0,), (0,)), ((), ()))


def mm(a, b, dims=NN):
    return lax.dot_general(a, b, dims, preferred_element_type=f32)


def halves(value):
    high = value.astype(bf16)
    return high, (value - high.astype(f32)).astype(bf16)


def iota(shape, dim):
    return lax.broadcasted_iota(jnp.int32, shape, dim)


def log_of(short):
    total = jnp.full_like(short, 1.0 / 7.0)
    for n in (6, 5, 4, 3, 2, 1):
        total = total * short + 1.0 / n
    return -short * total


def by_pole(ref, level, shape):
    place = iota(shape, 0) % POLES
    value = jnp.full(shape, ref[level, POLES - 1], f32)
    for k in range(POLES - 1):
        value = jnp.where(place == k, ref[level, k], value)
    return value


def couplings(short, decay, weight, shift):
    gain = jnp.sqrt(1.0 - decay * decay)
    forward, backward = weight * gain, weight * short
    sum_f = jnp.zeros_like(short)
    sum_b = jnp.zeros_like(short)
    for m in range(POLES):
        short_m, f_m, b_m = (short, forward, backward) if m == 0 else tuple(shift(t, m) for t in (short, forward, backward))
        share = 1.0 / (short + short_m - short * short_m)
        sum_f += b_m * share
        sum_b += f_m * share
    return forward, sum_b, forward * sum_f, backward * sum_b


def line_tables(pole_ref, weight_ref, level):
    shape = (8, 128)
    decay, weight = by_pole(pole_ref, level, shape), by_pole(weight_ref, level, shape)
    short = 1.0 - decay
    rate = log_of(short)
    _, _, c_f, c_b = couplings(short, decay, weight, lambda t, m: pltpu.roll(t, m, 0))
    forward = iota((8, BLOCK), 0) < POLES
    place = iota((8, BLOCK), 1)
    wide = lambda t: jnp.concatenate([t, t], axis=1)
    summary = jnp.exp(wide(rate) * jnp.where(forward, BLOCK - 1 - place, place).astype(f32))
    entry = jnp.exp(wide(rate) * jnp.where(forward, place + 1, BLOCK - place).astype(f32))
    entry = entry * jnp.where(forward, wide(c_f), wide(c_b))
    return rate, c_f, c_b, summary, entry


def toeplitz(rate, low, up, store):
    shape = (8, 128)
    sub, lane = iota(shape, 0), iota(shape, 1)
    apart = (sub - lane).astype(f32)
    rates = [jnp.broadcast_to(rate[k : k + 1, :], shape) for k in range(POLES)]
    step = [jnp.exp(8.0 * r) for r in rates]
    below = [jnp.broadcast_to(low[k : k + 1, :], shape) * jnp.exp(rates[k] * apart) for k in range(POLES)]
    above = [jnp.broadcast_to(up[k : k + 1, :], shape) * jnp.exp(rates[k] * (-120.0 - apart)) for k in range(POLES)]
    upper = {}
    for m in range(15, -17, -1):
        upper[m] = (above[0] + above[1]) + (above[2] + above[3])
        above = [a * s for a, s in zip(above, step)]
    tiles = {}
    for m in range(-16, 32):
        if m < 0:
            tiles[m] = upper[m]
            continue
        lower = (below[0] + below[1]) + (below[2] + below[3])
        below = [b * s for b, s in zip(below, step)]
        tiles[m] = lower if m > 15 else jnp.where(sub + 8 * m >= lane, lower, upper[m])
    for m in range(-16, 32, 2):
        high, low_part = halves(jnp.concatenate([tiles[m], tiles[m + 1]], axis=0))
        for j in range(2):
            if 0 <= m + 16 * j < 32:
                store(8 * (m + 16 * j), 128 * j, high, low_part)


def end_mix(pole_ref, weight_ref, level, shape):
    decay, weight = by_pole(pole_ref, level, shape), by_pole(weight_ref, level, shape)
    short = 1.0 - decay
    parts, total = [], jnp.zeros(shape, f32)
    for k in range(POLES):
        p_k = jnp.full(shape, pole_ref[level, k], f32)
        q_k = 1.0 - p_k
        part = weight_ref[level, k] * jnp.sqrt(1.0 - p_k * p_k) / (short + q_k - short * q_k)
        total += part
        parts.append(part * p_k)
    return [-part / total for part in parts], log_of(short)


def scan_blocks(inputs, decay, mix):
    forward = iota(decay.shape, 0) < POLES
    state = jnp.zeros_like(decay)
    before = []
    for block in inputs:
        before.append(state)
        state = decay * state + block
    end = jnp.zeros_like(decay)
    for k in range(POLES):
        end += mix[k] * jnp.broadcast_to(state[k : k + 1, :], decay.shape)
    state = end
    out = [None] * len(inputs)
    for i in range(len(inputs) - 1, -1, -1):
        out[i] = jnp.where(forward, before[i], state)
        state = decay * state + inputs[i]
    return out


def kernel_states(
    px, wx, py, wy, u_hbm, p_hbm, left_out, right_out,
    u_v, zh_v, zl_v, ty_v, txh_v, txl_v, sx_v, sxh_v, sxl_v, ex_v, ey_v, decay_y, v_v, ys_v,
    row_out, row_in, col_out, col_in, row_out2, row_in2, col_out2, col_in2,
    load_sem, save_sem, row_send, row_recv, col_send, col_recv, row_send2, row_recv2, col_send2, col_recv2,
):
    r, c = lax.axis_index("row"), lax.axis_index("col")
    load = lambda l: pltpu.make_async_copy(u_hbm.at[l], u_v.at[l], load_sem.at[l])
    save = lambda l: pltpu.make_async_copy(u_v.at[l], p_hbm.at[l], save_sem.at[l])

    @pl.loop(0, LEVELS)
    def _(l):
        load(l).start()

    barrier = pltpu.get_barrier_semaphore()

    @pl.loop(1, PEERS)
    def _(j):
        pl.semaphore_signal(barrier, inc=1, device_id=(lax.rem(r + j, PEERS), c), device_id_type=MESH)
        pl.semaphore_signal(barrier, inc=1, device_id=(r, lax.rem(c + j, PEERS)), device_id_type=MESH)

    tile = (8, 128)

    @pl.loop(0, LEVELS)
    def _(l):
        rate, c_f, c_b, summary, entry = line_tables(px, wx, l)
        s_h, s_l = halves(summary)
        sx_v[l] = jnp.concatenate([s_h.astype(f32), s_l.astype(f32)], axis=0).astype(bf16)
        sxh_v[pl.ds(8 * l, 8), :] = s_h.astype(f32)
        sxl_v[pl.ds(8 * l, 8), :] = s_l.astype(f32)
        ex_v[l] = entry

        def store_x(row, lane, high, low):
            txh_v[l, row : row + 16, lane : lane + 128] = high
            txl_v[l, row : row + 16, lane : lane + 128] = low

        toeplitz(rate, c_b, c_f, store_x)

        rate, c_f, c_b, summary, entry = line_tables(py, wy, l)
        s_h, s_l = halves(summary)
        ty_v[l, 256:272, :] = jnp.concatenate([s_h.astype(f32), s_l.astype(f32)], axis=0).astype(bf16)
        ey_v[l] = entry
        decay_y[l] = jnp.exp(rate * BLOCK)

        def store_y(row, lane, high, low):
            ty_v[l, row : row + 16, lane : lane + 128] = high
            ty_v[l, row + 272 : row + 288, lane : lane + 128] = low

        toeplitz(rate, c_f, c_b, store_y)

    forward_wide = iota((8, BLOCK), 0) < POLES

    @pl.loop(0, LEVELS)
    def _(l):
        load(l).wait()
        sums = []
        for s in range(2):
            rows = slice(BLOCK * s, BLOCK * (s + 1))
            u_h, u_l = halves(u_v[l, rows, :])
            d1 = mm(ty_v[l], u_h)
            d2 = mm(ty_v[l, 0:272, :], u_l)
            z = d1[0:256] + d1[272:528] + d2[0:256]
            v = d1[256:264] + d1[264:272] + d2[256:264]
            z_h, z_l = halves(z)
            zh_v[l, rows, :] = z_h
            zl_v[l, rows, :] = z_l
            e1 = mm(sx_v[l], z_h, NT)
            e2 = mm(sx_v[l], z_l, NT)
            row_out[2 * l + s, :, 0:256] = e1[0:8] + e1[8:16] + e2[0:8]
            v_v[s * LEVELS + l] = v
            sums.append(v)
        v_h, v_l = halves(jnp.concatenate(sums, axis=0))
        y1 = mm(jnp.concatenate([v_h, v_l], axis=0), txh_v[l])
        y2 = mm(v_h, txl_v[l])
        ys = y1[0:16] + y1[16:32] + y2
        ys_v[l] = ys
        decay = jnp.concatenate([decay_y[l], decay_y[l]], axis=1)
        both = jnp.where(forward_wide, decay * ys[0:8] + ys[8:16], ys[0:8] + decay * ys[8:16])
        col_out[2 * l] = both[:, 0:128]
        col_out[2 * l + 1] = both[:, 128:256]

    v_h, v_l = halves(v_v[...].reshape(128, BLOCK))
    sxh = jnp.concatenate([sxh_v[...], sxh_v[...]], axis=0).astype(bf16)
    sxl = jnp.concatenate([sxl_v[...], sxl_v[...]], axis=0).astype(bf16)
    corner = mm(v_h, sxh, NT) + (mm(v_l, sxh, NT) + mm(v_h, sxl, NT))
    own = iota((128, 128), 0) // 8 == iota((128, 128), 1) // 8
    corner = jnp.sum(jnp.where(own, corner, 0.0).reshape(16, 8, 128), axis=0)

    @pl.loop(0, PEERS)
    def _(q):
        row_out[q, :, 256:384] = corner

    pl.semaphore_wait(barrier, 2 * (PEERS - 1))

    def row_copy(peer, there, src, dst, send, recv):
        return pltpu.make_async_remote_copy(
            src_ref=src.at[peer], dst_ref=dst.at[there], send_sem=send.at[peer], recv_sem=recv.at[there],
            device_id=(peer, c), device_id_type=MESH,
        )

    def col_copy(peer, there, src, dst, send, recv):
        return pltpu.make_async_remote_copy(
            src_ref=src.at[peer], dst_ref=dst.at[there], send_sem=send.at[peer], recv_sem=recv.at[there],
            device_id=(r, peer), device_id_type=MESH,
        )

    row1 = (row_out, row_in, row_send, row_recv)
    col1 = (col_out, col_in, col_send, col_recv)
    row2 = (row_out2, row_in2, row_send2, row_recv2)
    col2 = (col_out2, col_in2, col_send2, col_recv2)

    @pl.loop(1, PEERS)
    def _(j):
        row_copy(lax.rem(r + j, PEERS), r, *row1).start()
        col_copy(lax.rem(c + j, PEERS), c, *col1).start()

    row_in[r] = row_out[r]
    col_in[c] = col_out[c]

    def local_field(l):
        p = mm(zh_v[l], txh_v[l]) + (mm(zl_v[l], txh_v[l]) + mm(zh_v[l], txl_v[l]))
        u_v[l] = p
        save(l).start()

    @pl.loop(0, LEVELS // 2)
    def _(l):
        local_field(l)

    sub, lane = iota(tile, 0), iota(tile, 1)
    level_of = (lane // 8) % LEVELS
    along_lanes = level_of * POLES + lane % POLES
    along_subs = level_of * POLES + sub % POLES

    def spread(ref, where_to):
        value = jnp.zeros(tile, f32)
        for n in range(LEVELS * POLES):
            value = jnp.where(where_to == n, ref[n // POLES, n % POLES], value)
        return value

    px_l, wx_l = spread(px, along_lanes), spread(wx, along_lanes)
    qx_l = 1.0 - px_l
    corner_decay_x = jnp.exp(log_of(qx_l) * BLOCK)
    square = (128, 128)
    stack = lambda t: jnp.concatenate([t] * 16, axis=0)
    p_c, q_c, g_c = stack(px_l), stack(qx_l), stack(wx_l * jnp.sqrt(1.0 - px_l * px_l))
    p_r, q_r, g_r = p_c.T, q_c.T, g_c.T
    row_id, lane_id = iota(square, 0), iota(square, 1)
    pair = (row_id // 8 == lane_id // 8) & (row_id % 8 < POLES) & (lane_id % 8 >= POLES)
    part = jnp.where(pair, g_r / (q_r + q_c - q_r * q_c), 0.0)
    total = jnp.sum(part, axis=0, keepdims=True)
    total = jnp.where(total > 0.0, total, 1.0)
    corner_mix_x = -(part * p_r) / total

    py_s, wy_s = spread(py, along_subs), spread(wy, along_subs)
    qy_s = 1.0 - py_s
    rate_y = log_of(qy_s)
    slab_decay_y, corner_decay_y = jnp.exp(rate_y * BLOCK), jnp.exp(rate_y * (2 * BLOCK))
    gy_s = wy_s * jnp.sqrt(1.0 - py_s * py_s)
    corner_mix_y, total = [], jnp.zeros(tile, f32)
    for k in range(POLES):
        row = lambda t: jnp.broadcast_to(t[k : k + 1, :], tile)
        q_k = row(qy_s)
        part = row(gy_s) / (qy_s + q_k - qy_s * q_k)
        total += part
        corner_mix_y.append(part * row(py_s))
    corner_mix_y = [-part / total for part in corner_mix_y]

    mix_x, rate_own = end_mix(px, wx, r // 2, (8, BLOCK))
    decay_own_x = jnp.exp(rate_own * BLOCK)
    mix_y, rate_own = end_mix(py, wy, c // 2, tile)
    decay_own_y = jnp.exp(rate_own * (2 * BLOCK))

    @pl.loop(1, PEERS)
    def _(j):
        peer = lax.rem(r + j, PEERS)
        row_copy(peer, peer, *row1).wait_recv()

    entering = scan_blocks([row_in[i, :, 0:256] for i in range(PEERS)], decay_own_x, mix_x)
    for i in range(PEERS):
        row_out2[i] = entering[i]

    @pl.loop(1, PEERS)
    def _(j):
        row_copy(lax.rem(r + j, PEERS), r, *row2).start()

    row_in2[r] = row_out2[r]

    mine = jnp.full(tile, r, jnp.int32)
    corners = [row_in[i, :, 256:384] for i in range(PEERS)]
    state, enter_f = jnp.zeros(tile, f32), jnp.zeros(tile, f32)
    for i in range(PEERS):
        enter_f = jnp.where(mine == i, state, enter_f)
        state = corner_decay_x * state + corners[i]
    state = lax.dot_general(state, corner_mix_x, NN, precision=lax.Precision.HIGHEST, preferred_element_type=f32)
    enter_b = jnp.zeros(tile, f32)
    for i in range(PEERS - 1, -1, -1):
        enter_b = jnp.where(mine == i, state, enter_b)
        state = corner_decay_x * state + corners[i]
    corner = jnp.where(lane % 8 < POLES, enter_f, enter_b)
    swapped = pltpu.roll(corner, 64, 1)
    first = jnp.where(lane < 64, corner, swapped)
    second = jnp.where(lane < 64, swapped, corner)
    forward = sub < POLES
    both = jnp.where(forward, slab_decay_y * first + second, first + slab_decay_y * second)

    @pl.loop(1, PEERS)
    def _(j):
        peer = lax.rem(c + j, PEERS)
        col_copy(peer, peer, *col1).wait_recv()

    entering = scan_blocks([col_in[i] for i in range(PEERS)], decay_own_y, mix_y)
    for i in range(PEERS):
        col_out2[i, 0:8, :] = entering[i]
        col_out2[i, 8:16, :] = both

    @pl.loop(1, PEERS)
    def _(j):
        col_copy(lax.rem(c + j, PEERS), c, *col2).start()

    col_in2[c] = col_out2[c]

    @pl.loop(LEVELS // 2, LEVELS)
    def _(l):
        local_field(l)

    @pl.loop(1, PEERS)
    def _(j):
        peer = lax.rem(c + j, PEERS)
        col_copy(peer, peer, *col2).wait_recv()

    mine = jnp.full(tile, c, jnp.int32)
    corners = [col_in2[i, 8:16, :] for i in range(PEERS)]
    state, enter_f = jnp.zeros(tile, f32), jnp.zeros(tile, f32)
    for i in range(PEERS):
        enter_f = jnp.where(mine == i, state, enter_f)
        state = corner_decay_y * state + corners[i]
    end = jnp.zeros(tile, f32)
    for k in range(POLES):
        end += corner_mix_y[k] * jnp.broadcast_to(state[k : k + 1, :], tile)
    state, enter_b = end, jnp.zeros(tile, f32)
    for i in range(PEERS - 1, -1, -1):
        enter_b = jnp.where(mine == i, state, enter_b)
        state = corner_decay_y * state + corners[i]
    corner_f = jnp.where(lane < 64, enter_f, slab_decay_y * enter_f + first)
    corner_b = jnp.where(lane < 64, slab_decay_y * enter_b + second, enter_b)
    corner = jnp.where(forward, corner_f, corner_b)

    spread_out = jnp.where(row_id // 8 == lane_id // 8, stack(corner), 0.0)
    k_h, k_l = halves(spread_out)
    ex_all = ex_v[...].reshape(64, BLOCK)
    x_h, x_l = halves(jnp.concatenate([ex_all, ex_all], axis=0))
    through = mm(k_h, x_h) + (mm(k_l, x_h) + mm(k_h, x_l))

    @pl.loop(1, PEERS)
    def _(j):
        peer = lax.rem(r + j, PEERS)
        row_copy(peer, peer, *row2).wait_recv()

    rounded = lambda t: t.astype(bf16).astype(f32)
    for l in range(LEVELS):
        decay = jnp.concatenate([decay_y[l], decay_y[l]], axis=1)
        enter = jnp.concatenate([col_in2[2 * l, 0:8, :], col_in2[2 * l + 1, 0:8, :]], axis=1)
        ys = ys_v[l]
        slabs = (
            jnp.where(forward_wide, enter, decay * enter + ys[8:16]),
            jnp.where(forward_wide, decay * enter + ys[0:8], enter),
        )
        x_h = rounded(ex_v[l])
        x_l = ex_v[l] - x_h
        y_h = rounded(ey_v[l])
        y_l = ey_v[l] - y_h
        for s in range(2):
            f = row_in2[2 * l + s]
            f_h = rounded(f)
            f_l = f - f_h
            at = 8 * (s * LEVELS + l)
            g = slabs[s] + through[at : at + 8]
            g_h = rounded(g)
            g_l = g - g_h
            left_out[2 * l + s] = jnp.concatenate([f_h, f_l, f_h, y_h, y_h, y_l], axis=0).astype(bf16)
            right_out[2 * l + s] = jnp.concatenate([x_h, x_h, x_l, g_h, g_l, g_h], axis=0).astype(bf16)

    @pl.loop(1, PEERS)
    def _(j):
        for peer, there, ends, make in (
            (lax.rem(r + j, PEERS), r, row1, row_copy), (lax.rem(r + j, PEERS), r, row2, row_copy),
            (lax.rem(c + j, PEERS), c, col1, col_copy), (lax.rem(c + j, PEERS), c, col2, col_copy),
        ):
            make(peer, there, *ends).wait_send()

    @pl.loop(0, LEVELS)
    def _(l):
        save(l).wait()


def kernel_field(p_ref, left_ref, right_ref, out_ref):
    for s in range(2):
        rows = slice(BLOCK * s, BLOCK * (s + 1))
        out_ref[0, rows, :] = jnp.exp(p_ref[0, rows, :] + mm(left_ref[s], right_ref[s], TN))


def on_device(source, pole_x, weight_x, pole_y, weight_y):
    smem = pl.BlockSpec(memory_space=pltpu.SMEM)
    vmem = pl.BlockSpec(memory_space=pltpu.VMEM)
    hbm = pl.BlockSpec(memory_space=pl.ANY)
    shape = source.shape
    V = pltpu.VMEM
    sems = pltpu.SemaphoreType.DMA((PEERS,))
    local, left, right = pl.pallas_call(
        kernel_states,
        out_shape=(
            jax.ShapeDtypeStruct(shape, f32),
            jax.ShapeDtypeStruct((16, 48, BLOCK), bf16),
            jax.ShapeDtypeStruct((16, 48, BLOCK), bf16),
        ),
        in_specs=[smem] * 4 + [hbm],
        out_specs=(hbm, vmem, vmem),
        scratch_shapes=[
            V(shape, f32), V(shape, bf16), V(shape, bf16),
            V((LEVELS, 528, BLOCK), bf16), V((LEVELS, BLOCK, BLOCK), bf16), V((LEVELS, BLOCK, BLOCK), bf16),
            V((LEVELS, 16, BLOCK), bf16), V((64, BLOCK), f32), V((64, BLOCK), f32),
            V((LEVELS, 8, BLOCK), f32), V((LEVELS, 8, BLOCK), f32), V((LEVELS, 8, 128), f32),
            V((16, 8, BLOCK), f32), V((LEVELS, 16, BLOCK), f32),
            V((PEERS, 8, 384), f32), V((PEERS, 8, 384), f32), V((PEERS, 8, 128), f32), V((PEERS, 8, 128), f32),
            V((PEERS, 8, BLOCK), f32), V((PEERS, 8, BLOCK), f32), V((PEERS, 16, 128), f32), V((PEERS, 16, 128), f32),
            pltpu.SemaphoreType.DMA((LEVELS,)), pltpu.SemaphoreType.DMA((LEVELS,)),
        ] + [sems] * 8,
        compiler_params=pltpu.CompilerParams(collective_id=0, has_side_effects=True, vmem_limit_bytes=48 * 2**20),
    )(pole_x, weight_x, pole_y, weight_y, source)
    field = pl.BlockSpec((1, 2 * BLOCK, BLOCK), lambda l: (l, 0, 0))
    ends = pl.BlockSpec((2, 48, BLOCK), lambda l: (l, 0, 0))
    return pl.pallas_call(
        kernel_field,
        out_shape=jax.ShapeDtypeStruct(shape, f32),
        grid=(LEVELS,),
        in_specs=[field, ends, ends],
        out_specs=field,
    )(local, left, right)


def solution(mesh):
    return jax.shard_map(
        on_device,
        mesh=mesh,
        in_specs=(P(None, "col", "row"), P(), P(), P(), P()),
        out_specs=P(None, "col", "row"),
        check_vma=False,
    )
```

time: 369 us -> 48.3 us (0.13)
  matrix products: 120 us -> 0 us
  local copies, waits for them, and re-layouts: 74.4 us -> 6.45 us
  waiting for transfers between devices: 65.5 us -> 0 us
  blocking collectives: 64.9 us -> 0 us
  Pallas kernels: 0 us -> 41.5 us
  other arithmetic: 19.7 us -> 0 us
  starting transfers between devices: 18.8 us -> 0 us
    dot_general x22 -> x0, matrix products: 120 us -> none  [the longest x2 32.6 us: line_local(): states = jnp.einsum('lkb,lmcb->lckm', state_map, blocked, precision=highest)]
    all_to_all x2 -> x0, waiting for transfers between devices: 65.5 us -> none  [the longest x1 48.6 us: on_device(): lax.all_to_all(source, 'row', split_axis=1, concat_axis=2, tiled=True)]
    all_gather x3 -> x0, blocking collectives: 64.9 us -> none  [prefix(): pieces = jax.tree.map(lambda part: lax.all_gather(part, axis), value)]
    pallas_call x0 -> x2, Pallas kernels: none -> 41.5 us  [the longest x1 33.9 us: on_device(): pl.pallas_call(kernel_states, out_shape=(jax.ShapeDtypeStruct(shape, f32)...]
    unnamed x18 -> x10, local copies, waits for them, and re-layouts: 37.9 us -> 6.45 us
    all_to_all x2 -> x0, starting transfers between devices: 18.8 us -> none  [the longest x1 10.8 us: on_device(): lax.all_to_all(smooth_lines, 'row', split_axis=2, concat_axis=1, tiled=True)]
    all_to_all x3 -> x0, local copies, waits for them, and re-layouts: 18.6 us -> none  [the longest x2 12 us: on_device(): lax.all_to_all(smooth_lines, 'row', split_axis=2, concat_axis=1, tiled=True)]
    reshape x2 -> x0, local copies, waits for them, and re-layouts: 14.2 us -> none  [the longest x1 9.44 us: line_finish(): return fixed.reshape(shape_out)]
  transfers between devices with their start and end apart: 2 -> 0, of which waited for: 2 -> 0; matrix products, arithmetic and copies ran while one was open for 7% -> 0% of each run, Pallas kernels for 0% -> 0%
where the time goes in v1:
time: 48.3 us; the launch traced here: 47.9 us
  Pallas kernels  41.5 us (86%)
  local copies, waits for them, and re-layouts  6.45 us (13%)
    pallas_call x1, Pallas kernels, on_device(): pl.pallas_call(kernel_states, out_shape=(jax.ShapeDtypeStruct(shape, f32)...  33.9 us
    pallas_call x1, Pallas kernels, on_device(): pl.pallas_call(kernel_field, out_shape=jax.ShapeDtypeStruct(shape, f32),...  7.58 us
    unnamed x10, local copies, waits for them, and re-layouts  6.45 us

profile of v1, /device:TPU:1, one launch (start us, length us, event | category | flops | bytes accessed | tf_op | source)
XLA Modules:
  0.0 47.9 jit_solution(8166158661224544035)
XLA Ops:
  0.0 0.8 %copy.6.px = f32[8,4]{1,0:T(8,128)S(1)} copy(f32[8,4]{0,1:T(4,128)} %param.6) | data formatting | bytes 256 | tf_op args[1]
  0.8 0.8 %copy.7.wx = f32[8,4]{1,0:T(8,128)S(1)} copy(f32[8,4]{0,1:T(4,128)} %param.7) | data formatting | bytes 256 | tf_op args[2]
  1.5 0.8 %copy.8.py = f32[8,4]{1,0:T(8,128)S(1)} copy(f32[8,4]{0,1:T(4,128)} %param.8) | data formatting | bytes 256 | tf_op args[3]
  2.3 0.8 %copy.9.wy = f32[8,4]{1,0:T(8,128)S(1)} copy(f32[8,4]{0,1:T(4,128)} %param.9) | data formatting | bytes 256 | tf_op args[4]
  3.0 33.9 %shard_map.55 = (f32[8,512,256]{2,1,0:T(8,128)S(1)}, bf16[16,48,256]{2,1,0:T(8,128)(2,1)S(1)}, bf16[16,48,256]{2,1,0:T(8,128)(2,1)S(1)}) custom-call(f32[8,4]{1,0:T(8,128)S(1)} %copy.6.px, f32[8,4]{1,0:T(8,128)S(1)} %copy.7.wx, f32[8,4]{1,0:T(8,128)S(1)} %copy.8.py, f32[8,4]{1,0:T(8,128)S(1)} %copy.9.wy, f32[8,512,256]{2,1,0:T(8,128)} %u_hbm.1), custom_call_target="tpu_custom_call" | custom-call | tf_op jit(solution)/shard_map/pallas_call | solution.py:444
  36.9 0.0 copy-start
  36.9 1.9 %copy-done = f32[8,512,256]{2,1,0:T(8,128)} copy-done((f32[8,512,256]{2,1,0:T(8,128)}, f32[8,512,256]{2,1,0:T(8,128)S(1)}, u32[]{:S(2)}) %copy-start) | copy-done | bytes 4194328
  38.9 0.0 copy-start.1
  38.9 0.7 %copy-done.1 = bf16[16,48,256]{2,1,0:T(8,128)(2,1)} copy-done((bf16[16,48,256]{2,1,0:T(8,128)(2,1)}, bf16[16,48,256]{2,1,0:T(8,128)(2,1)S(1)}, u32[]{:S(2)}) %copy-start.1) | copy-done | bytes 393240
  39.6 0.0 copy-start.2
  39.6 0.7 %copy-done.2 = bf16[16,48,256]{2,1,0:T(8,128)(2,1)} copy-done((bf16[16,48,256]{2,1,0:T(8,128)(2,1)}, bf16[16,48,256]{2,1,0:T(8,128)(2,1)S(1)}, u32[]{:S(2)}) %copy-start.2) | copy-done | bytes 393240
  40.4 7.6 %shard_map.56 = f32[8,512,256]{2,1,0:T(8,128)} custom-call(f32[8,512,256]{2,1,0:T(8,128)} %copy-done, bf16[16,48,256]{2,1,0:T(8,128)(2,1)} %copy-done.1, bf16[16,48,256]{2,1,0:T(8,128)(2,1)} %copy-done.2), custom_call_target="tpu_custom_call" | custom-call | tf_op jit(solution)/shard_map/pallas_call | solution.py:467
Async XLA Ops:
  36.9 1.9 %copy-start = (f32[8,512,256]{2,1,0:T(8,128)}, f32[8,512,256]{2,1,0:T(8,128)S(1)}, u32[]{:S(2)}) copy-start(f32[8,512,256]{2,1,0:T(8,128)S(1)} %get-tuple-element.8.p_ref) | copy-start | bytes 12582916
  38.9 0.7 %copy-start.1 = (bf16[16,48,256]{2,1,0:T(8,128)(2,1)}, bf16[16,48,256]{2,1,0:T(8,128)(2,1)S(1)}, u32[]{:S(2)}) copy-start(bf16[16,48,256]{2,1,0:T(8,128)(2,1)S(1)} %get-tuple-element.9.left_ref) | copy-start | bytes 1179652
  39.6 0.7 %copy-start.2 = (bf16[16,48,256]{2,1,0:T(8,128)(2,1)}, bf16[16,48,256]{2,1,0:T(8,128)(2,1)S(1)}, u32[]{:S(2)}) copy-start(bf16[16,48,256]{2,1,0:T(8,128)(2,1)S(1)} %get-tuple-element.10.right_ref) | copy-start | bytes 1179652

commit v2 on v1

--- a/solution.py
+++ b/solution.py
@@ -12,6 +12,7 @@
 POLES = 4
 BLOCK = 256
 PEERS = 16
+GROUPS = ((0, 1, 2, 3), (4, 5, 6, 7))
 f32 = jnp.float32
 bf16 = jnp.bfloat16
 NN = (((1,), (0,)), ((), ()))
@@ -41,9 +42,9 @@
 
 def by_pole(ref, level, shape):
     place = iota(shape, 0) % POLES
-    value = jnp.full(shape, ref[level, POLES - 1], f32)
+    value = jnp.full(shape, ref[POLES - 1, level], f32)
     for k in range(POLES - 1):
-        value = jnp.where(place == k, ref[level, k], value)
+        value = jnp.where(place == k, ref[k, level], value)
     return value
 
 
@@ -107,9 +108,9 @@
     short = 1.0 - decay
     parts, total = [], jnp.zeros(shape, f32)
     for k in range(POLES):
-        p_k = jnp.full(shape, pole_ref[level, k], f32)
+        p_k = jnp.full(shape, pole_ref[k, level], f32)
         q_k = 1.0 - p_k
-        part = weight_ref[level, k] * jnp.sqrt(1.0 - p_k * p_k) / (short + q_k - short * q_k)
+        part = weight_ref[k, level] * jnp.sqrt(1.0 - p_k * p_k) / (short + q_k - short * q_k)
         total += part
         parts.append(part * p_k)
     return [-part / total for part in parts], log_of(short)
@@ -134,14 +135,20 @@
 
 
 def kernel_states(
-    px, wx, py, wy, u_hbm, p_hbm, left_out, right_out,
-    u_v, zh_v, zl_v, ty_v, txh_v, txl_v, sx_v, sxh_v, sxl_v, ex_v, ey_v, decay_y, v_v, ys_v,
+    px_hbm, wx_hbm, py_hbm, wy_hbm, u_hbm, p_out, left_out, right_out,
+    px, wx, py, wy, u_v, zh_v, zl_v, ty_v, txh_v, txl_v, sx_v, sxh_v, sxl_v, ex_v, ey_v, decay_y, v_v,
     row_out, row_in, col_out, col_in, row_out2, row_in2, col_out2, col_in2,
-    load_sem, save_sem, row_send, row_recv, col_send, col_recv, row_send2, row_recv2, col_send2, col_recv2,
+    table_sem, load_sem, row_send, row_recv, col_send, col_recv, row_send2, row_recv2, col_send2, col_recv2,
 ):
     r, c = lax.axis_index("row"), lax.axis_index("col")
     load = lambda l: pltpu.make_async_copy(u_hbm.at[l], u_v.at[l], load_sem.at[l])
-    save = lambda l: pltpu.make_async_copy(u_v.at[l], p_hbm.at[l], save_sem.at[l])
+
+    tables = [
+        pltpu.make_async_copy(src, dst, table_sem.at[n])
+        for n, (src, dst) in enumerate(((px_hbm, px), (wx_hbm, wx), (py_hbm, py), (wy_hbm, wy)))
+    ]
+    for table in tables:
+        table.start()
 
     @pl.loop(0, LEVELS)
     def _(l):
@@ -155,21 +162,18 @@
         pl.semaphore_signal(barrier, inc=1, device_id=(r, lax.rem(c + j, PEERS)), device_id_type=MESH)
 
     tile = (8, 128)
-
-    @pl.loop(0, LEVELS)
-    def _(l):
+    for table in tables:
+        table.wait()
+
+    toeplitz_x = []
+    for l in range(LEVELS):
         rate, c_f, c_b, summary, entry = line_tables(px, wx, l)
         s_h, s_l = halves(summary)
         sx_v[l] = jnp.concatenate([s_h.astype(f32), s_l.astype(f32)], axis=0).astype(bf16)
         sxh_v[pl.ds(8 * l, 8), :] = s_h.astype(f32)
         sxl_v[pl.ds(8 * l, 8), :] = s_l.astype(f32)
         ex_v[l] = entry
-
-        def store_x(row, lane, high, low):
-            txh_v[l, row : row + 16, lane : lane + 128] = high
-            txl_v[l, row : row + 16, lane : lane + 128] = low
-
-        toeplitz(rate, c_b, c_f, store_x)
+        toeplitz_x.append((rate, c_b, c_f))
 
         rate, c_f, c_b, summary, entry = line_tables(py, wy, l)
         s_h, s_l = halves(summary)
@@ -185,9 +189,7 @@
 
     forward_wide = iota((8, BLOCK), 0) < POLES
 
-    @pl.loop(0, LEVELS)
-    def _(l):
-        load(l).wait()
+    def column_products(l):
         sums = []
         for s in range(2):
             rows = slice(BLOCK * s, BLOCK * (s + 1))
@@ -199,20 +201,31 @@
             z_h, z_l = halves(z)
             zh_v[l, rows, :] = z_h
             zl_v[l, rows, :] = z_l
-            e1 = mm(sx_v[l], z_h, NT)
-            e2 = mm(sx_v[l], z_l, NT)
-            row_out[2 * l + s, :, 0:256] = e1[0:8] + e1[8:16] + e2[0:8]
             v_v[s * LEVELS + l] = v
             sums.append(v)
-        v_h, v_l = halves(jnp.concatenate(sums, axis=0))
-        y1 = mm(jnp.concatenate([v_h, v_l], axis=0), txh_v[l])
-        y2 = mm(v_h, txl_v[l])
-        ys = y1[0:16] + y1[16:32] + y2
-        ys_v[l] = ys
         decay = jnp.concatenate([decay_y[l], decay_y[l]], axis=1)
-        both = jnp.where(forward_wide, decay * ys[0:8] + ys[8:16], ys[0:8] + decay * ys[8:16])
+        both = jnp.where(forward_wide, decay * sums[0] + sums[1], sums[0] + decay * sums[1])
         col_out[2 * l] = both[:, 0:128]
         col_out[2 * l + 1] = both[:, 128:256]
+
+    def row_states(l):
+        for s in range(2):
+            rows = slice(BLOCK * s, BLOCK * (s + 1))
+            e1 = mm(sx_v[l], zh_v[l, rows, :], NT)
+            e2 = mm(sx_v[l], zl_v[l, rows, :], NT)
+            row_out[2 * l + s, :, 0:256] = e1[0:8] + e1[8:16] + e2[0:8]
+
+    ready = []
+    for group in GROUPS:
+        for l in group:
+            load(l).wait()
+        for l in group:
+            column_products(l)
+        for l in ready:
+            row_states(l)
+        ready = group
+    for l in ready:
+        row_states(l)
 
     v_h, v_l = halves(v_v[...].reshape(128, BLOCK))
     sxh = jnp.concatenate([sxh_v[...], sxh_v[...]], axis=0).astype(bf16)
@@ -252,13 +265,19 @@
     row_in[r] = row_out[r]
     col_in[c] = col_out[c]
 
+    for l in range(LEVELS):
+
+        def store_x(row, lane, high, low):
+            txh_v[l, row : row + 16, lane : lane + 128] = high
+            txl_v[l, row : row + 16, lane : lane + 128] = low
+
+        toeplitz(*toeplitz_x[l], store_x)
+
     def local_field(l):
         p = mm(zh_v[l], txh_v[l]) + (mm(zl_v[l], txh_v[l]) + mm(zh_v[l], txl_v[l]))
-        u_v[l] = p
-        save(l).start()
-
-    @pl.loop(0, LEVELS // 2)
-    def _(l):
+        p_out[l] = p
+
+    for l in range(LEVELS // 2):
         local_field(l)
 
     sub, lane = iota(tile, 0), iota(tile, 1)
@@ -269,7 +288,7 @@
     def spread(ref, where_to):
         value = jnp.zeros(tile, f32)
         for n in range(LEVELS * POLES):
-            value = jnp.where(where_to == n, ref[n // POLES, n % POLES], value)
+            value = jnp.where(where_to == n, ref[n % POLES, n // POLES], value)
         return value
 
     px_l, wx_l = spread(px, along_lanes), spread(wx, along_lanes)
@@ -354,8 +373,7 @@
 
     col_in2[c] = col_out2[c]
 
-    @pl.loop(LEVELS // 2, LEVELS)
-    def _(l):
+    for l in range(LEVELS // 2, LEVELS):
         local_field(l)
 
     @pl.loop(1, PEERS)
@@ -395,11 +413,13 @@
     for l in range(LEVELS):
         decay = jnp.concatenate([decay_y[l], decay_y[l]], axis=1)
         enter = jnp.concatenate([col_in2[2 * l, 0:8, :], col_in2[2 * l + 1, 0:8, :]], axis=1)
-        ys = ys_v[l]
         slabs = (
-            jnp.where(forward_wide, enter, decay * enter + ys[8:16]),
-            jnp.where(forward_wide, decay * enter + ys[0:8], enter),
+            jnp.where(forward_wide, enter, decay * enter + v_v[LEVELS + l]),
+            jnp.where(forward_wide, decay * enter + v_v[l], enter),
         )
+        e_h, e_l = halves(jnp.concatenate(slabs, axis=0))
+        wide = mm(jnp.concatenate([e_h, e_l], axis=0), txh_v[l])
+        wide = wide[0:16] + wide[16:32] + mm(e_h, txl_v[l])
         x_h = rounded(ex_v[l])
         x_l = ex_v[l] - x_h
         y_h = rounded(ey_v[l])
@@ -409,7 +429,7 @@
             f_h = rounded(f)
             f_l = f - f_h
             at = 8 * (s * LEVELS + l)
-            g = slabs[s] + through[at : at + 8]
+            g = wide[8 * s : 8 * s + 8] + through[at : at + 8]
             g_h = rounded(g)
             g_l = g - g_h
             left_out[2 * l + s] = jnp.concatenate([f_h, f_l, f_h, y_h, y_h, y_l], axis=0).astype(bf16)
@@ -423,21 +443,24 @@
         ):
             make(peer, there, *ends).wait_send()
 
+
+def kernel_field(p_ref, left_ref, right_ref, out_hbm, out_v, save_sem):
+    save = lambda l: pltpu.make_async_copy(out_v.at[l], out_hbm.at[l], save_sem.at[l])
+
+    for l in range(LEVELS):
+        for s in range(2):
+            rows = slice(BLOCK * s, BLOCK * (s + 1))
+            out_v[l, rows, :] = jnp.exp(p_ref[l, rows, :] + mm(left_ref[2 * l + s], right_ref[2 * l + s], TN))
+        save(l).start()
+
     @pl.loop(0, LEVELS)
     def _(l):
         save(l).wait()
 
 
-def kernel_field(p_ref, left_ref, right_ref, out_ref):
-    for s in range(2):
-        rows = slice(BLOCK * s, BLOCK * (s + 1))
-        out_ref[0, rows, :] = jnp.exp(p_ref[0, rows, :] + mm(left_ref[s], right_ref[s], TN))
-
-
 def on_device(source, pole_x, weight_x, pole_y, weight_y):
-    smem = pl.BlockSpec(memory_space=pltpu.SMEM)
     vmem = pl.BlockSpec(memory_space=pltpu.VMEM)
-    hbm = pl.BlockSpec(memory_space=pl.ANY)
+    hbm = pl.BlockSpec(memory_space=pltpu.HBM)
     shape = source.shape
     V = pltpu.VMEM
     sems = pltpu.SemaphoreType.DMA((PEERS,))
@@ -448,28 +471,27 @@
             jax.ShapeDtypeStruct((16, 48, BLOCK), bf16),
             jax.ShapeDtypeStruct((16, 48, BLOCK), bf16),
         ),
-        in_specs=[smem] * 4 + [hbm],
-        out_specs=(hbm, vmem, vmem),
-        scratch_shapes=[
+        in_specs=[hbm] * 5,
+        out_specs=(vmem, vmem, vmem),
+        scratch_shapes=[pltpu.SMEM((POLES, LEVELS), f32)] * 4 + [
             V(shape, f32), V(shape, bf16), V(shape, bf16),
             V((LEVELS, 528, BLOCK), bf16), V((LEVELS, BLOCK, BLOCK), bf16), V((LEVELS, BLOCK, BLOCK), bf16),
             V((LEVELS, 16, BLOCK), bf16), V((64, BLOCK), f32), V((64, BLOCK), f32),
             V((LEVELS, 8, BLOCK), f32), V((LEVELS, 8, BLOCK), f32), V((LEVELS, 8, 128), f32),
-            V((16, 8, BLOCK), f32), V((LEVELS, 16, BLOCK), f32),
+            V((16, 8, BLOCK), f32),
             V((PEERS, 8, 384), f32), V((PEERS, 8, 384), f32), V((PEERS, 8, 128), f32), V((PEERS, 8, 128), f32),
             V((PEERS, 8, BLOCK), f32), V((PEERS, 8, BLOCK), f32), V((PEERS, 16, 128), f32), V((PEERS, 16, 128), f32),
-            pltpu.SemaphoreType.DMA((LEVELS,)), pltpu.SemaphoreType.DMA((LEVELS,)),
+            pltpu.SemaphoreType.DMA((4,)), pltpu.SemaphoreType.DMA((LEVELS,)),
         ] + [sems] * 8,
         compiler_params=pltpu.CompilerParams(collective_id=0, has_side_effects=True, vmem_limit_bytes=48 * 2**20),
-    )(pole_x, weight_x, pole_y, weight_y, source)
-    field = pl.BlockSpec((1, 2 * BLOCK, BLOCK), lambda l: (l, 0, 0))
-    ends = pl.BlockSpec((2, 48, BLOCK), lambda l: (l, 0, 0))
+    )(*(pltpu.with_memory_space_constraint(t.T, pltpu.HBM) for t in (pole_x, weight_x, pole_y, weight_y)), source)
     return pl.pallas_call(
         kernel_field,
         out_shape=jax.ShapeDtypeStruct(shape, f32),
-        grid=(LEVELS,),
-        in_specs=[field, ends, ends],
-        out_specs=field,
+        in_specs=[vmem] * 3,
+        out_specs=hbm,
+        scratch_shapes=[V(shape, f32), pltpu.SemaphoreType.DMA((LEVELS,))],
+        compiler_params=pltpu.CompilerParams(vmem_limit_bytes=24 * 2**20),
     )(local, left, right)
 
 

time: 48.3 us -> 29.8 us (0.62)
  Pallas kernels: 41.5 us -> 29.7 us
  local copies, waits for them, and re-layouts: 6.45 us -> 0 us
    pallas_call x1, Pallas kernels: 33.9 us -> 27.4 us  [on_device(): pl.pallas_call(kernel_states, out_shape=(jax.ShapeDtypeStruct(shape, f32)...]
    unnamed x10 -> x0, local copies, waits for them, and re-layouts: 6.45 us -> none
    pallas_call x1, Pallas kernels: 7.58 us -> 2.36 us  [on_device(): pl.pallas_call(kernel_field, out_shape=jax.ShapeDtypeStruct(shape, f32),...]
where the time goes in v2:
time: 29.8 us; the launch traced here: 29.7 us
  Pallas kernels  29.7 us (100%)
    pallas_call x1, Pallas kernels, on_device(): pl.pallas_call(kernel_states, out_shape=(jax.ShapeDtypeStruct(shape, f32)...  27.4 us
    pallas_call x1, Pallas kernels, on_device(): pl.pallas_call(kernel_field, out_shape=jax.ShapeDtypeStruct(shape, f32),...  2.36 us

profile of v2, /device:TPU:1, one launch (start us, length us, event | category | flops | bytes accessed | tf_op | source)
XLA Modules:
  0.0 29.7 jit_solution(403442981255007755)
XLA Ops:
  0.0 27.4 %shard_map.55 = (f32[8,512,256]{2,1,0:T(8,128)S(1)}, bf16[16,48,256]{2,1,0:T(8,128)(2,1)S(1)}, bf16[16,48,256]{2,1,0:T(8,128)(2,1)S(1)}) custom-call(f32[4,8]{1,0:T(4,128)} %bitcast.4, f32[4,8]{1,0:T(4,128)} %bitcast.5, f32[4,8]{1,0:T(4,128)} %bitcast.6, f32[4,8]{1,0:T(4,128)} %bitcast.7, f32[8,512,256]{2,1,0:T(8,128)} %u_hbm.1), custom_call_target="tpu_custom_call" | custom-call | tf_op jit(solution)/shard_map/pallas_call | solution.py:467
  27.4 2.4 %shard_map.56 = f32[8,512,256]{2,1,0:T(8,128)} custom-call(f32[8,512,256]{2,1,0:T(8,128)S(1)} %get-tuple-element.8.p_ref, bf16[16,48,256]{2,1,0:T(8,128)(2,1)S(1)} %get-tuple-element.9.left_ref, bf16[16,48,256]{2,1,0:T(8,128)(2,1)S(1)} %get-tuple-element.10.right_ref), custom_call_target="tpu_custom_call" | custom-call | tf_op jit(solution)/shard_map/pallas_call | solution.py:488

commit v3 on v2

--- a/solution.py
+++ b/solution.py
@@ -12,6 +12,7 @@
 POLES = 4
 BLOCK = 256
 PEERS = 16
+EARLY = 2
 GROUPS = ((0, 1, 2, 3), (4, 5, 6, 7))
 f32 = jnp.float32
 bf16 = jnp.bfloat16
@@ -136,7 +137,7 @@
 
 def kernel_states(
     px_hbm, wx_hbm, py_hbm, wy_hbm, u_hbm, p_out, left_out, right_out,
-    px, wx, py, wy, u_v, zh_v, zl_v, ty_v, txh_v, txl_v, sx_v, sxh_v, sxl_v, ex_v, ey_v, decay_y, v_v,
+    px, wx, py, wy, u_v, uh_v, ul_v, zh_v, zl_v, ty_v, sy_v, txh_v, txl_v, sx_v, sxh_v, sxl_v, ex_v, ey_v, decay_y, v_v,
     row_out, row_in, col_out, col_in, row_out2, row_in2, col_out2, col_in2,
     table_sem, load_sem, row_send, row_recv, col_send, col_recv, row_send2, row_recv2, col_send2, col_recv2,
 ):
@@ -165,7 +166,7 @@
     for table in tables:
         table.wait()
 
-    toeplitz_x = []
+    toeplitz_x, toeplitz_y = [], []
     for l in range(LEVELS):
         rate, c_f, c_b, summary, entry = line_tables(px, wx, l)
         s_h, s_l = halves(summary)
@@ -177,30 +178,23 @@
 
         rate, c_f, c_b, summary, entry = line_tables(py, wy, l)
         s_h, s_l = halves(summary)
-        ty_v[l, 256:272, :] = jnp.concatenate([s_h.astype(f32), s_l.astype(f32)], axis=0).astype(bf16)
+        sy_v[l] = jnp.concatenate([s_h.astype(f32), s_l.astype(f32)], axis=0).astype(bf16)
         ey_v[l] = entry
         decay_y[l] = jnp.exp(rate * BLOCK)
-
-        def store_y(row, lane, high, low):
-            ty_v[l, row : row + 16, lane : lane + 128] = high
-            ty_v[l, row + 272 : row + 288, lane : lane + 128] = low
-
-        toeplitz(rate, c_f, c_b, store_y)
+        toeplitz_y.append((rate, c_f, c_b))
 
     forward_wide = iota((8, BLOCK), 0) < POLES
 
-    def column_products(l):
+    def column_states(l):
         sums = []
         for s in range(2):
             rows = slice(BLOCK * s, BLOCK * (s + 1))
             u_h, u_l = halves(u_v[l, rows, :])
-            d1 = mm(ty_v[l], u_h)
-            d2 = mm(ty_v[l, 0:272, :], u_l)
-            z = d1[0:256] + d1[272:528] + d2[0:256]
-            v = d1[256:264] + d1[264:272] + d2[256:264]
-            z_h, z_l = halves(z)
-            zh_v[l, rows, :] = z_h
-            zl_v[l, rows, :] = z_l
+            uh_v[l, rows, :] = u_h
+            ul_v[l, rows, :] = u_l
+            d1 = mm(sy_v[l], u_h)
+            d2 = mm(sy_v[l], u_l)
+            v = d1[0:8] + d1[8:16] + d2[0:8]
             v_v[s * LEVELS + l] = v
             sums.append(v)
         decay = jnp.concatenate([decay_y[l], decay_y[l]], axis=1)
@@ -211,21 +205,17 @@
     def row_states(l):
         for s in range(2):
             rows = slice(BLOCK * s, BLOCK * (s + 1))
-            e1 = mm(sx_v[l], zh_v[l, rows, :], NT)
-            e2 = mm(sx_v[l], zl_v[l, rows, :], NT)
+            e1 = mm(sx_v[l], uh_v[l, rows, :], NT)
+            e2 = mm(sx_v[l], ul_v[l, rows, :], NT)
             row_out[2 * l + s, :, 0:256] = e1[0:8] + e1[8:16] + e2[0:8]
 
-    ready = []
     for group in GROUPS:
         for l in group:
             load(l).wait()
         for l in group:
-            column_products(l)
-        for l in ready:
+            column_states(l)
+        for l in group:
             row_states(l)
-        ready = group
-    for l in ready:
-        row_states(l)
 
     v_h, v_l = halves(v_v[...].reshape(128, BLOCK))
     sxh = jnp.concatenate([sxh_v[...], sxh_v[...]], axis=0).astype(bf16)
@@ -247,8 +237,9 @@
         )
 
     def col_copy(peer, there, src, dst, send, recv):
+        rows = pl.ds(0, 8 if src is col_out else 12)
         return pltpu.make_async_remote_copy(
-            src_ref=src.at[peer], dst_ref=dst.at[there], send_sem=send.at[peer], recv_sem=recv.at[there],
+            src_ref=src.at[peer, rows], dst_ref=dst.at[there, rows], send_sem=send.at[peer], recv_sem=recv.at[there],
             device_id=(r, peer), device_id_type=MESH,
         )
 
@@ -267,17 +258,30 @@
 
     for l in range(LEVELS):
 
+        def store_y(row, lane, high, low):
+            ty_v[l, row : row + 16, lane : lane + 128] = high
+            ty_v[l, row + 256 : row + 272, lane : lane + 128] = low
+
         def store_x(row, lane, high, low):
             txh_v[l, row : row + 16, lane : lane + 128] = high
             txl_v[l, row : row + 16, lane : lane + 128] = low
 
+        toeplitz(*toeplitz_y[l], store_y)
         toeplitz(*toeplitz_x[l], store_x)
 
+    for l in range(LEVELS):
+        for s in range(2):
+            rows = slice(BLOCK * s, BLOCK * (s + 1))
+            d1 = mm(ty_v[l], uh_v[l, rows, :])
+            d2 = mm(ty_v[l, 0:256, :], ul_v[l, rows, :])
+            z_h, z_l = halves(d1[0:256] + d1[256:512] + d2)
+            zh_v[l, rows, :] = z_h
+            zl_v[l, rows, :] = z_l
+
     def local_field(l):
-        p = mm(zh_v[l], txh_v[l]) + (mm(zl_v[l], txh_v[l]) + mm(zh_v[l], txl_v[l]))
-        p_out[l] = p
-
-    for l in range(LEVELS // 2):
+        p_out[l] = mm(zh_v[l], txh_v[l]) + (mm(zl_v[l], txh_v[l]) + mm(zh_v[l], txl_v[l]))
+
+    for l in range(EARLY):
         local_field(l)
 
     sub, lane = iota(tile, 0), iota(tile, 1)
@@ -330,8 +334,11 @@
         row_copy(peer, peer, *row1).wait_recv()
 
     entering = scan_blocks([row_in[i, :, 0:256] for i in range(PEERS)], decay_own_x, mix_x)
+    f_h, f_l = halves(jnp.concatenate(entering, axis=0))
+    high = mm(jnp.concatenate([f_h, f_l], axis=0), ty_v[r // 2, 0:256, :], NT)
+    through = high[0:128] + (high[128:256] + mm(f_h, ty_v[r // 2, 256:512, :], NT))
     for i in range(PEERS):
-        row_out2[i] = entering[i]
+        row_out2[i] = through[8 * i : 8 * i + 8]
 
     @pl.loop(1, PEERS)
     def _(j):
@@ -357,6 +364,8 @@
     forward = sub < POLES
     both = jnp.where(forward, slab_decay_y * first + second, first + slab_decay_y * second)
 
+    packed = jnp.where(lane < 64, both, pltpu.roll(both, POLES, 0))[0:POLES]
+
     @pl.loop(1, PEERS)
     def _(j):
         peer = lax.rem(c + j, PEERS)
@@ -365,15 +374,15 @@
     entering = scan_blocks([col_in[i] for i in range(PEERS)], decay_own_y, mix_y)
     for i in range(PEERS):
         col_out2[i, 0:8, :] = entering[i]
-        col_out2[i, 8:16, :] = both
+        col_out2[i, 8:12, :] = packed
 
     @pl.loop(1, PEERS)
     def _(j):
         col_copy(lax.rem(c + j, PEERS), c, *col2).start()
 
-    col_in2[c] = col_out2[c]
-
-    for l in range(LEVELS // 2, LEVELS):
+    col_in2[c, 0:12, :] = col_out2[c, 0:12, :]
+
+    for l in range(EARLY, LEVELS):
         local_field(l)
 
     @pl.loop(1, PEERS)
@@ -381,19 +390,25 @@
         peer = lax.rem(c + j, PEERS)
         col_copy(peer, peer, *col2).wait_recv()
 
-    mine = jnp.full(tile, c, jnp.int32)
-    corners = [col_in2[i, 8:16, :] for i in range(PEERS)]
-    state, enter_f = jnp.zeros(tile, f32), jnp.zeros(tile, f32)
+    half = (POLES, 128)
+    mine = jnp.full(half, c, jnp.int32)
+    corners = [col_in2[i, 8:12, :] for i in range(PEERS)]
+    decay = corner_decay_y[0:POLES]
+    state, enter_f = jnp.zeros(half, f32), jnp.zeros(half, f32)
     for i in range(PEERS):
         enter_f = jnp.where(mine == i, state, enter_f)
-        state = corner_decay_y * state + corners[i]
-    end = jnp.zeros(tile, f32)
+        state = decay * state + corners[i]
+    end = jnp.zeros(half, f32)
     for k in range(POLES):
-        end += corner_mix_y[k] * jnp.broadcast_to(state[k : k + 1, :], tile)
-    state, enter_b = end, jnp.zeros(tile, f32)
+        end += corner_mix_y[k][0:POLES] * jnp.broadcast_to(state[k : k + 1, :], half)
+    turn = lambda t: pltpu.roll(jnp.concatenate([t, t], axis=0), 64, 1)
+    state, enter_b = turn(end)[0:POLES], jnp.zeros(half, f32)
     for i in range(PEERS - 1, -1, -1):
         enter_b = jnp.where(mine == i, state, enter_b)
-        state = corner_decay_y * state + corners[i]
+        state = decay * state + corners[i]
+    twice = lambda t: jnp.concatenate([t, t], axis=0)
+    enter_f = jnp.where(lane < 64, twice(enter_f), turn(enter_f))
+    enter_b = jnp.where(lane < 64, turn(enter_b), twice(enter_b))
     corner_f = jnp.where(lane < 64, enter_f, slab_decay_y * enter_f + first)
     corner_b = jnp.where(lane < 64, slab_decay_y * enter_b + second, enter_b)
     corner = jnp.where(forward, corner_f, corner_b)
@@ -474,8 +489,8 @@
         in_specs=[hbm] * 5,
         out_specs=(vmem, vmem, vmem),
         scratch_shapes=[pltpu.SMEM((POLES, LEVELS), f32)] * 4 + [
-            V(shape, f32), V(shape, bf16), V(shape, bf16),
-            V((LEVELS, 528, BLOCK), bf16), V((LEVELS, BLOCK, BLOCK), bf16), V((LEVELS, BLOCK, BLOCK), bf16),
+            V(shape, f32), V(shape, bf16), V(shape, bf16), V(shape, bf16), V(shape, bf16),
+            V((LEVELS, 512, BLOCK), bf16), V((LEVELS, 16, BLOCK), bf16), V((LEVELS, BLOCK, BLOCK), bf16), V((LEVELS, BLOCK, BLOCK), bf16),
             V((LEVELS, 16, BLOCK), bf16), V((64, BLOCK), f32), V((64, BLOCK), f32),
             V((LEVELS, 8, BLOCK), f32), V((LEVELS, 8, BLOCK), f32), V((LEVELS, 8, 128), f32),
             V((16, 8, BLOCK), f32),

time: 29.8 us -> 28 us (0.940)
  Pallas kernels: 29.7 us -> 28 us
    pallas_call x1, Pallas kernels: 27.4 us -> 25.6 us  [on_device(): pl.pallas_call(kernel_states, out_shape=(jax.ShapeDtypeStruct(shape, f32)...]
where the time goes in v3:
time: 28 us
  Pallas kernels  28 us (100%)
    pallas_call x1, Pallas kernels, on_device(): pl.pallas_call(kernel_states, out_shape=(jax.ShapeDtypeStruct(shape, f32)...  25.6 us
    pallas_call x1, Pallas kernels, on_device(): pl.pallas_call(kernel_field, out_shape=jax.ShapeDtypeStruct(shape, f32),...  2.35 us

profile of v3, /device:TPU:1, one launch (start us, length us, event | category | flops | bytes accessed | tf_op | source)
XLA Modules:
  0.0 28.0 jit_solution(8328858054465687924)
XLA Ops:
  0.0 25.6 %shard_map.55 = (f32[8,512,256]{2,1,0:T(8,128)S(1)}, bf16[16,48,256]{2,1,0:T(8,128)(2,1)S(1)}, bf16[16,48,256]{2,1,0:T(8,128)(2,1)S(1)}) custom-call(f32[4,8]{1,0:T(4,128)} %bitcast.4, f32[4,8]{1,0:T(4,128)} %bitcast.5, f32[4,8]{1,0:T(4,128)} %bitcast.6, f32[4,8]{1,0:T(4,128)} %bitcast.7, f32[8,512,256]{2,1,0:T(8,128)} %u_hbm.1), custom_call_target="tpu_custom_call" | custom-call | tf_op jit(solution)/shard_map/pallas_call | solution.py:482
  25.6 2.4 %shard_map.56 = f32[8,512,256]{2,1,0:T(8,128)} custom-call(f32[8,512,256]{2,1,0:T(8,128)S(1)} %get-tuple-element.8.p_ref, bf16[16,48,256]{2,1,0:T(8,128)(2,1)S(1)} %get-tuple-element.9.left_ref, bf16[16,48,256]{2,1,0:T(8,128)(2,1)S(1)} %get-tuple-element.10.right_ref), custom_call_target="tpu_custom_call" | custom-call | tf_op jit(solution)/shard_map/pallas_call | solution.py:503

commit v4 on v3

--- a/solution.py
+++ b/solution.py
@@ -13,7 +13,7 @@
 BLOCK = 256
 PEERS = 16
 EARLY = 2
-GROUPS = ((0, 1, 2, 3), (4, 5, 6, 7))
+GROUPS = ((0, 1, 2), (3, 4, 5), (6, 7))
 f32 = jnp.float32
 bf16 = jnp.bfloat16
 NN = (((1,), (0,)), ((), ()))
@@ -135,6 +135,18 @@
     return out
 
 
+def row_peers(r):
+    reach = (0, 1, 2, 1)
+    steps = [(dx, dy) for dx in range(4) for dy in range(4) if dx or dy]
+    steps.sort(key=lambda d: -(reach[d[0]] + reach[d[1]]))
+    return [lax.rem(r // 4 + dx, 4) * 4 + lax.rem(lax.rem(r, 4) + dy, 4) for dx, dy in steps]
+
+
+def col_peers(c):
+    steps = [(dz, core) for dz in (4, 3, 5, 2, 6, 1, 7, 0) for core in (0, 1) if dz or core]
+    return [lax.rem(c // 2 + dz, 8) * 2 + lax.rem(lax.rem(c, 2) + core, 2) for dz, core in steps]
+
+
 def kernel_states(
     px_hbm, wx_hbm, py_hbm, wy_hbm, u_hbm, p_out, left_out, right_out,
     px, wx, py, wy, u_v, uh_v, ul_v, zh_v, zl_v, ty_v, sy_v, txh_v, txl_v, sx_v, sxh_v, sxl_v, ex_v, ey_v, decay_y, v_v,
@@ -248,10 +260,10 @@
     row2 = (row_out2, row_in2, row_send2, row_recv2)
     col2 = (col_out2, col_in2, col_send2, col_recv2)
 
-    @pl.loop(1, PEERS)
-    def _(j):
-        row_copy(lax.rem(r + j, PEERS), r, *row1).start()
-        col_copy(lax.rem(c + j, PEERS), c, *col1).start()
+    rows_to, cols_to = row_peers(r), col_peers(c)
+    for row_peer, col_peer in zip(rows_to, cols_to):
+        row_copy(row_peer, r, *row1).start()
+        col_copy(col_peer, c, *col1).start()
 
     row_in[r] = row_out[r]
     col_in[c] = col_out[c]
@@ -328,23 +340,8 @@
     mix_y, rate_own = end_mix(py, wy, c // 2, tile)
     decay_own_y = jnp.exp(rate_own * (2 * BLOCK))
 
-    @pl.loop(1, PEERS)
-    def _(j):
-        peer = lax.rem(r + j, PEERS)
+    for peer in rows_to:
         row_copy(peer, peer, *row1).wait_recv()
-
-    entering = scan_blocks([row_in[i, :, 0:256] for i in range(PEERS)], decay_own_x, mix_x)
-    f_h, f_l = halves(jnp.concatenate(entering, axis=0))
-    high = mm(jnp.concatenate([f_h, f_l], axis=0), ty_v[r // 2, 0:256, :], NT)
-    through = high[0:128] + (high[128:256] + mm(f_h, ty_v[r // 2, 256:512, :], NT))
-    for i in range(PEERS):
-        row_out2[i] = through[8 * i : 8 * i + 8]
-
-    @pl.loop(1, PEERS)
-    def _(j):
-        row_copy(lax.rem(r + j, PEERS), r, *row2).start()
-
-    row_in2[r] = row_out2[r]
 
     mine = jnp.full(tile, r, jnp.int32)
     corners = [row_in[i, :, 256:384] for i in range(PEERS)]
@@ -366,9 +363,7 @@
 
     packed = jnp.where(lane < 64, both, pltpu.roll(both, POLES, 0))[0:POLES]
 
-    @pl.loop(1, PEERS)
-    def _(j):
-        peer = lax.rem(c + j, PEERS)
+    for peer in cols_to:
         col_copy(peer, peer, *col1).wait_recv()
 
     entering = scan_blocks([col_in[i] for i in range(PEERS)], decay_own_y, mix_y)
@@ -376,18 +371,34 @@
         col_out2[i, 0:8, :] = entering[i]
         col_out2[i, 8:12, :] = packed
 
-    @pl.loop(1, PEERS)
-    def _(j):
-        col_copy(lax.rem(c + j, PEERS), c, *col2).start()
+    for peer in cols_to:
+        col_copy(peer, c, *col2).start()
 
     col_in2[c, 0:12, :] = col_out2[c, 0:12, :]
+
+    entering = scan_blocks([row_in[i, :, 0:256] for i in range(PEERS)], decay_own_x, mix_x)
+    f_h, f_l = halves(jnp.concatenate(entering, axis=0))
+    high = mm(jnp.concatenate([f_h, f_l], axis=0), ty_v[r // 2, 0:256, :], NT)
+    through = high[0:128] + (high[128:256] + mm(f_h, ty_v[r // 2, 256:512, :], NT))
+    for i in range(PEERS):
+        row_out2[i] = through[8 * i : 8 * i + 8]
+
+    for peer in rows_to:
+        row_copy(peer, r, *row2).start()
+
+    row_in2[r] = row_out2[r]
+
+    for row_peer, col_peer in zip(rows_to, cols_to):
+        row_copy(row_peer, r, *row1).wait_send()
+        col_copy(col_peer, c, *col1).wait_send()
 
     for l in range(EARLY, LEVELS):
         local_field(l)
 
-    @pl.loop(1, PEERS)
-    def _(j):
-        peer = lax.rem(c + j, PEERS)
+    for row_peer, col_peer in zip(rows_to, cols_to):
+        row_copy(row_peer, r, *row2).wait_send()
+        col_copy(col_peer, c, *col2).wait_send()
+    for peer in cols_to:
         col_copy(peer, peer, *col2).wait_recv()
 
     half = (POLES, 128)
@@ -419,11 +430,6 @@
     x_h, x_l = halves(jnp.concatenate([ex_all, ex_all], axis=0))
     through = mm(k_h, x_h) + (mm(k_l, x_h) + mm(k_h, x_l))
 
-    @pl.loop(1, PEERS)
-    def _(j):
-        peer = lax.rem(r + j, PEERS)
-        row_copy(peer, peer, *row2).wait_recv()
-
     rounded = lambda t: t.astype(bf16).astype(f32)
     for l in range(LEVELS):
         decay = jnp.concatenate([decay_y[l], decay_y[l]], axis=1)
@@ -437,26 +443,24 @@
         wide = wide[0:16] + wide[16:32] + mm(e_h, txl_v[l])
         x_h = rounded(ex_v[l])
         x_l = ex_v[l] - x_h
+        for s in range(2):
+            at = 8 * (s * LEVELS + l)
+            g = wide[8 * s : 8 * s + 8] + through[at : at + 8]
+            g_h = rounded(g)
+            g_l = g - g_h
+            right_out[2 * l + s] = jnp.concatenate([x_h, x_h, x_l, g_h, g_l, g_h], axis=0).astype(bf16)
+
+    for peer in rows_to:
+        row_copy(peer, peer, *row2).wait_recv()
+
+    for l in range(LEVELS):
         y_h = rounded(ey_v[l])
         y_l = ey_v[l] - y_h
         for s in range(2):
             f = row_in2[2 * l + s]
             f_h = rounded(f)
             f_l = f - f_h
-            at = 8 * (s * LEVELS + l)
-            g = wide[8 * s : 8 * s + 8] + through[at : at + 8]
-            g_h = rounded(g)
-            g_l = g - g_h
             left_out[2 * l + s] = jnp.concatenate([f_h, f_l, f_h, y_h, y_h, y_l], axis=0).astype(bf16)
-            right_out[2 * l + s] = jnp.concatenate([x_h, x_h, x_l, g_h, g_l, g_h], axis=0).astype(bf16)
-
-    @pl.loop(1, PEERS)
-    def _(j):
-        for peer, there, ends, make in (
-            (lax.rem(r + j, PEERS), r, row1, row_copy), (lax.rem(r + j, PEERS), r, row2, row_copy),
-            (lax.rem(c + j, PEERS), c, col1, col_copy), (lax.rem(c + j, PEERS), c, col2, col_copy),
-        ):
-            make(peer, there, *ends).wait_send()
 
 
 def kernel_field(p_ref, left_ref, right_ref, out_hbm, out_v, save_sem):

time: 28 us -> 26.1 us (0.932)
  Pallas kernels: 28 us -> 26 us
    pallas_call x1, Pallas kernels: 25.6 us -> 23.6 us  [on_device(): pl.pallas_call(kernel_states, out_shape=(jax.ShapeDtypeStruct(shape, f32)...]
where the time goes in v4:
time: 26.1 us; the launch traced here: 26 us
  Pallas kernels  26 us (100%)
    pallas_call x1, Pallas kernels, on_device(): pl.pallas_call(kernel_states, out_shape=(jax.ShapeDtypeStruct(shape, f32)...  23.6 us
    pallas_call x1, Pallas kernels, on_device(): pl.pallas_call(kernel_field, out_shape=jax.ShapeDtypeStruct(shape, f32),...  2.36 us

profile of v4, /device:TPU:1, one launch (start us, length us, event | category | flops | bytes accessed | tf_op | source)
XLA Modules:
  0.0 26.0 jit_solution(16172859168223462649)
XLA Ops:
  0.0 23.6 %shard_map.55 = (f32[8,512,256]{2,1,0:T(8,128)S(1)}, bf16[16,48,256]{2,1,0:T(8,128)(2,1)S(1)}, bf16[16,48,256]{2,1,0:T(8,128)(2,1)S(1)}) custom-call(f32[4,8]{1,0:T(4,128)} %bitcast.4, f32[4,8]{1,0:T(4,128)} %bitcast.5, f32[4,8]{1,0:T(4,128)} %bitcast.6, f32[4,8]{1,0:T(4,128)} %bitcast.7, f32[8,512,256]{2,1,0:T(8,128)} %u_hbm.1), custom_call_target="tpu_custom_call" | custom-call | tf_op jit(solution)/shard_map/pallas_call | solution.py:486
  23.6 2.4 %shard_map.56 = f32[8,512,256]{2,1,0:T(8,128)} custom-call(f32[8,512,256]{2,1,0:T(8,128)S(1)} %get-tuple-element.8.p_ref, bf16[16,48,256]{2,1,0:T(8,128)(2,1)S(1)} %get-tuple-element.9.left_ref, bf16[16,48,256]{2,1,0:T(8,128)(2,1)S(1)} %get-tuple-element.10.right_ref), custom_call_target="tpu_custom_call" | custom-call | tf_op jit(solution)/shard_map/pallas_call | solution.py:507

commit v5 on v4

--- a/solution.py
+++ b/solution.py
@@ -117,22 +117,44 @@
     return [-part / total for part in parts], log_of(short)
 
 
-def scan_blocks(inputs, decay, mix):
+def powers_of(decay):
+    powers = [jnp.ones_like(decay)]
+    for _ in range(PEERS - 1):
+        powers.append(powers[-1] * decay)
+    return powers[::-1]
+
+
+def scan_blocks(inputs, decay, mix, powers):
     forward = iota(decay.shape, 0) < POLES
-    state = jnp.zeros_like(decay)
-    before = []
-    for block in inputs:
-        before.append(state)
-        state = decay * state + block
+    ahead, back = jnp.zeros_like(decay), jnp.zeros_like(decay)
+    before, behind = [], []
+    for i in range(len(inputs)):
+        before.append(ahead)
+        behind.append(back)
+        ahead = decay * ahead + inputs[i]
+        back = decay * back + inputs[-1 - i]
     end = jnp.zeros_like(decay)
     for k in range(POLES):
-        end += mix[k] * jnp.broadcast_to(state[k : k + 1, :], decay.shape)
-    state = end
-    out = [None] * len(inputs)
-    for i in range(len(inputs) - 1, -1, -1):
-        out[i] = jnp.where(forward, before[i], state)
-        state = decay * state + inputs[i]
-    return out
+        end += mix[k] * jnp.broadcast_to(ahead[k : k + 1, :], decay.shape)
+    return [jnp.where(forward, f, b + w * end) for f, b, w in zip(before, behind[::-1], powers)]
+
+
+def entry_weights(rate, span, here, forward):
+    here = here.astype(f32)
+    enter, end = [], []
+    for i in range(PEERS):
+        ahead, back = here - 1.0 - i, i - here - 1.0
+        distance = jnp.where(forward, ahead, back)
+        enter.append(jnp.where(distance >= 0.0, jnp.exp(rate * (span * jnp.maximum(distance, 0.0))), 0.0))
+        end.append(jnp.exp(rate * (span * (PEERS - 1.0 - i))))
+    return enter, end, jnp.where(forward, 0.0, jnp.exp(rate * (span * (PEERS - 1.0 - here))))
+
+
+def weighted(blocks, weights):
+    terms = [b * w for b, w in zip(blocks, weights)]
+    while len(terms) > 1:
+        terms = [terms[n] + terms[n + 1] for n in range(0, len(terms), 2)]
+    return terms[0]
 
 
 def row_peers(r):
@@ -221,24 +243,25 @@
             e2 = mm(sx_v[l], ul_v[l, rows, :], NT)
             row_out[2 * l + s, :, 0:256] = e1[0:8] + e1[8:16] + e2[0:8]
 
+    def corner_states():
+        v_h, v_l = halves(v_v[...].reshape(128, BLOCK))
+        sxh = jnp.concatenate([sxh_v[...], sxh_v[...]], axis=0).astype(bf16)
+        sxl = jnp.concatenate([sxl_v[...], sxl_v[...]], axis=0).astype(bf16)
+        corner = mm(v_h, sxh, NT) + (mm(v_l, sxh, NT) + mm(v_h, sxl, NT))
+        own = iota((128, 128), 0) // 8 == iota((128, 128), 1) // 8
+        corner = jnp.sum(jnp.where(own, corner, 0.0).reshape(16, 8, 128), axis=0)
+        for q in range(PEERS):
+            row_out[q, :, 256:384] = corner
+
     for group in GROUPS:
         for l in group:
             load(l).wait()
         for l in group:
             column_states(l)
+        if group is GROUPS[-1]:
+            corner_states()
         for l in group:
             row_states(l)
-
-    v_h, v_l = halves(v_v[...].reshape(128, BLOCK))
-    sxh = jnp.concatenate([sxh_v[...], sxh_v[...]], axis=0).astype(bf16)
-    sxl = jnp.concatenate([sxl_v[...], sxl_v[...]], axis=0).astype(bf16)
-    corner = mm(v_h, sxh, NT) + (mm(v_l, sxh, NT) + mm(v_h, sxl, NT))
-    own = iota((128, 128), 0) // 8 == iota((128, 128), 1) // 8
-    corner = jnp.sum(jnp.where(own, corner, 0.0).reshape(16, 8, 128), axis=0)
-
-    @pl.loop(0, PEERS)
-    def _(q):
-        row_out[q, :, 256:384] = corner
 
     pl.semaphore_wait(barrier, 2 * (PEERS - 1))
 
@@ -309,7 +332,7 @@
 
     px_l, wx_l = spread(px, along_lanes), spread(wx, along_lanes)
     qx_l = 1.0 - px_l
-    corner_decay_x = jnp.exp(log_of(qx_l) * BLOCK)
+    enter_x, end_x, back_x = entry_weights(log_of(qx_l), float(BLOCK), jnp.full(tile, r, jnp.int32), lane % 8 < POLES)
     square = (128, 128)
     stack = lambda t: jnp.concatenate([t] * 16, axis=0)
     p_c, q_c, g_c = stack(px_l), stack(qx_l), stack(wx_l * jnp.sqrt(1.0 - px_l * px_l))
@@ -320,11 +343,19 @@
     total = jnp.sum(part, axis=0, keepdims=True)
     total = jnp.where(total > 0.0, total, 1.0)
     corner_mix_x = -(part * p_r) / total
+    roll_mix_x = [
+        jnp.broadcast_to(jnp.sum(jnp.where(row_id == lane_id - d, corner_mix_x, 0.0), axis=0, keepdims=True), tile)
+        for d in range(1, 8)
+    ]
 
     py_s, wy_s = spread(py, along_subs), spread(wy, along_subs)
     qy_s = 1.0 - py_s
     rate_y = log_of(qy_s)
-    slab_decay_y, corner_decay_y = jnp.exp(rate_y * BLOCK), jnp.exp(rate_y * (2 * BLOCK))
+    slab_decay_y = jnp.exp(rate_y * BLOCK)
+    half = (POLES, 128)
+    enter_y, end_y, back_y = entry_weights(
+        rate_y[0:POLES], 2.0 * BLOCK, jnp.full(half, c, jnp.int32), iota(half, 1) < 64
+    )
     gy_s = wy_s * jnp.sqrt(1.0 - py_s * py_s)
     corner_mix_y, total = [], jnp.zeros(tile, f32)
     for k in range(POLES):
@@ -339,22 +370,15 @@
     decay_own_x = jnp.exp(rate_own * BLOCK)
     mix_y, rate_own = end_mix(py, wy, c // 2, tile)
     decay_own_y = jnp.exp(rate_own * (2 * BLOCK))
+    powers_x, powers_y = powers_of(decay_own_x), powers_of(decay_own_y)
 
     for peer in rows_to:
         row_copy(peer, peer, *row1).wait_recv()
 
-    mine = jnp.full(tile, r, jnp.int32)
     corners = [row_in[i, :, 256:384] for i in range(PEERS)]
-    state, enter_f = jnp.zeros(tile, f32), jnp.zeros(tile, f32)
-    for i in range(PEERS):
-        enter_f = jnp.where(mine == i, state, enter_f)
-        state = corner_decay_x * state + corners[i]
-    state = lax.dot_general(state, corner_mix_x, NN, precision=lax.Precision.HIGHEST, preferred_element_type=f32)
-    enter_b = jnp.zeros(tile, f32)
-    for i in range(PEERS - 1, -1, -1):
-        enter_b = jnp.where(mine == i, state, enter_b)
-        state = corner_decay_x * state + corners[i]
-    corner = jnp.where(lane % 8 < POLES, enter_f, enter_b)
+    end = weighted(corners, end_x)
+    end = weighted([pltpu.roll(end, d, 1) for d in range(1, 8)] + [jnp.zeros(tile, f32)], roll_mix_x + [end])
+    corner = weighted(corners, enter_x) + back_x * end
     swapped = pltpu.roll(corner, 64, 1)
     first = jnp.where(lane < 64, corner, swapped)
     second = jnp.where(lane < 64, swapped, corner)
@@ -366,7 +390,7 @@
     for peer in cols_to:
         col_copy(peer, peer, *col1).wait_recv()
 
-    entering = scan_blocks([col_in[i] for i in range(PEERS)], decay_own_y, mix_y)
+    entering = scan_blocks([col_in[i] for i in range(PEERS)], decay_own_y, mix_y, powers_y)
     for i in range(PEERS):
         col_out2[i, 0:8, :] = entering[i]
         col_out2[i, 8:12, :] = packed
@@ -376,7 +400,7 @@
 
     col_in2[c, 0:12, :] = col_out2[c, 0:12, :]
 
-    entering = scan_blocks([row_in[i, :, 0:256] for i in range(PEERS)], decay_own_x, mix_x)
+    entering = scan_blocks([row_in[i, :, 0:256] for i in range(PEERS)], decay_own_x, mix_x, powers_x)
     f_h, f_l = halves(jnp.concatenate(entering, axis=0))
     high = mm(jnp.concatenate([f_h, f_l], axis=0), ty_v[r // 2, 0:256, :], NT)
     through = high[0:128] + (high[128:256] + mm(f_h, ty_v[r // 2, 256:512, :], NT))
@@ -401,25 +425,16 @@
     for peer in cols_to:
         col_copy(peer, peer, *col2).wait_recv()
 
-    half = (POLES, 128)
-    mine = jnp.full(half, c, jnp.int32)
     corners = [col_in2[i, 8:12, :] for i in range(PEERS)]
-    decay = corner_decay_y[0:POLES]
-    state, enter_f = jnp.zeros(half, f32), jnp.zeros(half, f32)
-    for i in range(PEERS):
-        enter_f = jnp.where(mine == i, state, enter_f)
-        state = decay * state + corners[i]
+    state = weighted(corners, end_y)
     end = jnp.zeros(half, f32)
     for k in range(POLES):
         end += corner_mix_y[k][0:POLES] * jnp.broadcast_to(state[k : k + 1, :], half)
     turn = lambda t: pltpu.roll(jnp.concatenate([t, t], axis=0), 64, 1)
-    state, enter_b = turn(end)[0:POLES], jnp.zeros(half, f32)
-    for i in range(PEERS - 1, -1, -1):
-        enter_b = jnp.where(mine == i, state, enter_b)
-        state = decay * state + corners[i]
+    enter = weighted(corners, enter_y) + back_y * turn(end)[0:POLES]
     twice = lambda t: jnp.concatenate([t, t], axis=0)
-    enter_f = jnp.where(lane < 64, twice(enter_f), turn(enter_f))
-    enter_b = jnp.where(lane < 64, turn(enter_b), twice(enter_b))
+    enter_f = jnp.where(lane < 64, twice(enter), turn(enter))
+    enter_b = jnp.where(lane < 64, turn(enter), twice(enter))
     corner_f = jnp.where(lane < 64, enter_f, slab_decay_y * enter_f + first)
     corner_b = jnp.where(lane < 64, slab_decay_y * enter_b + second, enter_b)
     corner = jnp.where(forward, corner_f, corner_b)

time: 26.1 us -> 25.7 us (0.985)
  Pallas kernels: 26 us -> 25.7 us
    pallas_call x1, Pallas kernels: 23.6 us -> 23.3 us  [on_device(): pl.pallas_call(kernel_states, out_shape=(jax.ShapeDtypeStruct(shape, f32)...]
where the time goes in v5:
time: 25.7 us
  Pallas kernels  25.7 us (100%)
    pallas_call x1, Pallas kernels, on_device(): pl.pallas_call(kernel_states, out_shape=(jax.ShapeDtypeStruct(shape, f32)...  23.3 us
    pallas_call x1, Pallas kernels, on_device(): pl.pallas_call(kernel_field, out_shape=jax.ShapeDtypeStruct(shape, f32),...  2.36 us

profile of v5, /device:TPU:1, one launch (start us, length us, event | category | flops | bytes accessed | tf_op | source)
XLA Modules:
  0.0 25.7 jit_solution(12368596491859307124)
XLA Ops:
  0.0 23.3 %shard_map.55 = (f32[8,512,256]{2,1,0:T(8,128)S(1)}, bf16[16,48,256]{2,1,0:T(8,128)(2,1)S(1)}, bf16[16,48,256]{2,1,0:T(8,128)(2,1)S(1)}) custom-call(f32[4,8]{1,0:T(4,128)} %bitcast.4, f32[4,8]{1,0:T(4,128)} %bitcast.5, f32[4,8]{1,0:T(4,128)} %bitcast.6, f32[4,8]{1,0:T(4,128)} %bitcast.7, f32[8,512,256]{2,1,0:T(8,128)} %u_hbm.1), custom_call_target="tpu_custom_call" | custom-call | tf_op jit(solution)/shard_map/pallas_call | solution.py:501
  23.3 2.4 %shard_map.56 = f32[8,512,256]{2,1,0:T(8,128)} custom-call(f32[8,512,256]{2,1,0:T(8,128)S(1)} %get-tuple-element.8.p_ref, bf16[16,48,256]{2,1,0:T(8,128)(2,1)S(1)} %get-tuple-element.9.left_ref, bf16[16,48,256]{2,1,0:T(8,128)(2,1)S(1)} %get-tuple-element.10.right_ref), custom_call_target="tpu_custom_call" | custom-call | tf_op jit(solution)/shard_map/pallas_call | solution.py:522

commit v6 on v5

--- a/solution.py
+++ b/solution.py
@@ -13,7 +13,7 @@
 BLOCK = 256
 PEERS = 16
 EARLY = 2
-GROUPS = ((0, 1, 2), (3, 4, 5), (6, 7))
+GROUPS = ((0, 1), (2, 3, 4), (5, 6, 7))
 f32 = jnp.float32
 bf16 = jnp.bfloat16
 NN = (((1,), (0,)), ((), ()))
@@ -172,8 +172,8 @@
 def kernel_states(
     px_hbm, wx_hbm, py_hbm, wy_hbm, u_hbm, p_out, left_out, right_out,
     px, wx, py, wy, u_v, uh_v, ul_v, zh_v, zl_v, ty_v, sy_v, txh_v, txl_v, sx_v, sxh_v, sxl_v, ex_v, ey_v, decay_y, v_v,
-    row_out, row_in, col_out, col_in, row_out2, row_in2, col_out2, col_in2,
-    table_sem, load_sem, row_send, row_recv, col_send, col_recv, row_send2, row_recv2, col_send2, col_recv2,
+    row_out, row_in, corner_out, corner_in, col_out, col_in, row_out2, row_in2, col_out2, col_in2,
+    table_sem, load_sem, row_send, row_recv, corner_send, corner_recv, col_send, col_recv, row_send2, row_recv2, col_send2, col_recv2,
 ):
     r, c = lax.axis_index("row"), lax.axis_index("col")
     load = lambda l: pltpu.make_async_copy(u_hbm.at[l], u_v.at[l], load_sem.at[l])
@@ -241,7 +241,7 @@
             rows = slice(BLOCK * s, BLOCK * (s + 1))
             e1 = mm(sx_v[l], uh_v[l, rows, :], NT)
             e2 = mm(sx_v[l], ul_v[l, rows, :], NT)
-            row_out[2 * l + s, :, 0:256] = e1[0:8] + e1[8:16] + e2[0:8]
+            row_out[2 * l + s] = e1[0:8] + e1[8:16] + e2[0:8]
 
     def corner_states():
         v_h, v_l = halves(v_v[...].reshape(128, BLOCK))
@@ -250,18 +250,17 @@
         corner = mm(v_h, sxh, NT) + (mm(v_l, sxh, NT) + mm(v_h, sxl, NT))
         own = iota((128, 128), 0) // 8 == iota((128, 128), 1) // 8
         corner = jnp.sum(jnp.where(own, corner, 0.0).reshape(16, 8, 128), axis=0)
-        for q in range(PEERS):
-            row_out[q, :, 256:384] = corner
-
-    for group in GROUPS:
+        corner_out[0] = corner
+
+    for n, group in enumerate(GROUPS):
         for l in group:
             load(l).wait()
         for l in group:
             column_states(l)
-        if group is GROUPS[-1]:
-            corner_states()
-        for l in group:
-            row_states(l)
+        if n >= 1:
+            for l in GROUPS[n - 1]:
+                row_states(l)
+    corner_states()
 
     pl.semaphore_wait(barrier, 2 * (PEERS - 1))
 
@@ -278,6 +277,12 @@
             device_id=(r, peer), device_id_type=MESH,
         )
 
+    def corner_copy(peer, there):
+        return pltpu.make_async_remote_copy(
+            src_ref=corner_out.at[0], dst_ref=corner_in.at[there], send_sem=corner_send.at[peer],
+            recv_sem=corner_recv.at[there], device_id=(peer, c), device_id_type=MESH,
+        )
+
     row1 = (row_out, row_in, row_send, row_recv)
     col1 = (col_out, col_in, col_send, col_recv)
     row2 = (row_out2, row_in2, row_send2, row_recv2)
@@ -285,9 +290,16 @@
 
     rows_to, cols_to = row_peers(r), col_peers(c)
     for row_peer, col_peer in zip(rows_to, cols_to):
-        row_copy(row_peer, r, *row1).start()
+        corner_copy(row_peer, r).start()
         col_copy(col_peer, c, *col1).start()
 
+    for l in GROUPS[-1]:
+        row_states(l)
+
+    for peer in rows_to:
+        row_copy(peer, r, *row1).start()
+
+    corner_in[r] = corner_out[0]
     row_in[r] = row_out[r]
     col_in[c] = col_out[c]
 
@@ -373,9 +385,9 @@
     powers_x, powers_y = powers_of(decay_own_x), powers_of(decay_own_y)
 
     for peer in rows_to:
-        row_copy(peer, peer, *row1).wait_recv()
-
-    corners = [row_in[i, :, 256:384] for i in range(PEERS)]
+        corner_copy(peer, peer).wait_recv()
+
+    corners = [corner_in[i] for i in range(PEERS)]
     end = weighted(corners, end_x)
     end = weighted([pltpu.roll(end, d, 1) for d in range(1, 8)] + [jnp.zeros(tile, f32)], roll_mix_x + [end])
     corner = weighted(corners, enter_x) + back_x * end
@@ -400,7 +412,10 @@
 
     col_in2[c, 0:12, :] = col_out2[c, 0:12, :]
 
-    entering = scan_blocks([row_in[i, :, 0:256] for i in range(PEERS)], decay_own_x, mix_x, powers_x)
+    for peer in rows_to:
+        row_copy(peer, peer, *row1).wait_recv()
+
+    entering = scan_blocks([row_in[i] for i in range(PEERS)], decay_own_x, mix_x, powers_x)
     f_h, f_l = halves(jnp.concatenate(entering, axis=0))
     high = mm(jnp.concatenate([f_h, f_l], axis=0), ty_v[r // 2, 0:256, :], NT)
     through = high[0:128] + (high[128:256] + mm(f_h, ty_v[r // 2, 256:512, :], NT))
@@ -414,6 +429,7 @@
 
     for row_peer, col_peer in zip(rows_to, cols_to):
         row_copy(row_peer, r, *row1).wait_send()
+        corner_copy(row_peer, r).wait_send()
         col_copy(col_peer, c, *col1).wait_send()
 
     for l in range(EARLY, LEVELS):
@@ -513,10 +529,10 @@
             V((LEVELS, 16, BLOCK), bf16), V((64, BLOCK), f32), V((64, BLOCK), f32),
             V((LEVELS, 8, BLOCK), f32), V((LEVELS, 8, BLOCK), f32), V((LEVELS, 8, 128), f32),
             V((16, 8, BLOCK), f32),
-            V((PEERS, 8, 384), f32), V((PEERS, 8, 384), f32), V((PEERS, 8, 128), f32), V((PEERS, 8, 128), f32),
+            V((PEERS, 8, BLOCK), f32), V((PEERS, 8, BLOCK), f32), V((1, 8, 128), f32), V((PEERS, 8, 128), f32), V((PEERS, 8, 128), f32), V((PEERS, 8, 128), f32),
             V((PEERS, 8, BLOCK), f32), V((PEERS, 8, BLOCK), f32), V((PEERS, 16, 128), f32), V((PEERS, 16, 128), f32),
             pltpu.SemaphoreType.DMA((4,)), pltpu.SemaphoreType.DMA((LEVELS,)),
-        ] + [sems] * 8,
+        ] + [sems] * 10,
         compiler_params=pltpu.CompilerParams(collective_id=0, has_side_effects=True, vmem_limit_bytes=48 * 2**20),
     )(*(pltpu.with_memory_space_constraint(t.T, pltpu.HBM) for t in (pole_x, weight_x, pole_y, weight_y)), source)
     return pl.pallas_call(

time: 25.7 us -> 25.4 us (0.988)
  Pallas kernels: 25.7 us -> 25.4 us
    pallas_call x1, Pallas kernels: 23.3 us -> 23 us  [on_device(): pl.pallas_call(kernel_states, out_shape=(jax.ShapeDtypeStruct(shape, f32)...]
where the time goes in v6:
time: 25.4 us
  Pallas kernels  25.4 us (100%)
    pallas_call x1, Pallas kernels, on_device(): pl.pallas_call(kernel_states, out_shape=(jax.ShapeDtypeStruct(shape, f32)...  23 us
    pallas_call x1, Pallas kernels, on_device(): pl.pallas_call(kernel_field, out_shape=jax.ShapeDtypeStruct(shape, f32),...  2.36 us

profile of v6, /device:TPU:1, one launch (start us, length us, event | category | flops | bytes accessed | tf_op | source)
XLA Modules:
  0.0 25.4 jit_solution(11942288503938243087)
XLA Ops:
  0.0 23.0 %shard_map.55 = (f32[8,512,256]{2,1,0:T(8,128)S(1)}, bf16[16,48,256]{2,1,0:T(8,128)(2,1)S(1)}, bf16[16,48,256]{2,1,0:T(8,128)(2,1)S(1)}) custom-call(f32[4,8]{1,0:T(4,128)} %bitcast.4, f32[4,8]{1,0:T(4,128)} %bitcast.5, f32[4,8]{1,0:T(4,128)} %bitcast.6, f32[4,8]{1,0:T(4,128)} %bitcast.7, f32[8,512,256]{2,1,0:T(8,128)} %u_hbm.1), custom_call_target="tpu_custom_call" | custom-call | tf_op jit(solution)/shard_map/pallas_call | solution.py:517
  23.0 2.4 %shard_map.56 = f32[8,512,256]{2,1,0:T(8,128)} custom-call(f32[8,512,256]{2,1,0:T(8,128)S(1)} %get-tuple-element.8.p_ref, bf16[16,48,256]{2,1,0:T(8,128)(2,1)S(1)} %get-tuple-element.9.left_ref, bf16[16,48,256]{2,1,0:T(8,128)(2,1)S(1)} %get-tuple-element.10.right_ref), custom_call_target="tpu_custom_call" | custom-call | tf_op jit(solution)/shard_map/pallas_call | solution.py:538
